TPU v7x, 256 devices: a whole 4x4x8 slice. The times are simulated.
256 devices in a mesh: dp: 16 (over x, y), tensor: 16 (over z, core).
Axes of the slice: x: 4, y: 4, z: 8, core: 2. Of those that a mesh axis runs over, the one named last changes fastest.
Arguments:
- activations: bfloat16 [4096, 16384], P('dp', 'tensor'), may hold values from -6 to 6
- angles: float32 [14, 8192], P(None, 'tensor'), may hold values from -3.140625 to 3.140625
- clip_bits: int32 [256, 16384], P('dp', 'tensor'), may hold values from 0 to 65535, as said below
- codes: bfloat16 [16384, 10240], P('tensor', 'dp'), may hold values from -127 to 127, as said below
- exponents: int32 [10240], replicated, may hold values from -16 to -13
- cotangent: bfloat16 [4096, 10240], P('dp', 'tensor'), may hold values from -6 to 6
Outputs:
- input_grad: bfloat16 [4096, 16384], P('dp', 'tensor')
- angle_grad: float32 [14, 8192], P(None, 'tensor')
Inputs may be any that keep to these rules, and one draw needn't show every extreme that they name: Bit k (0 to 15) of clip_bits[w, i] is the clip mask of token 16 w + k at feature i; higher bits are zero. `codes`: every entry is a whole number.
All inputs are finite; a program needn't handle non-finite values.
Results may differ from a plain program's by a relative error of at most 0.003.
Values may be sent and summed in bfloat16 or wider, within the bound.
A program may use at most 128 MiB of HBM per device.

v0:
```python
import jax
import jax.numpy as jnp
from jax import lax
from jax.sharding import PartitionSpec as P


def partner(value, axis, apart):
    mask = 2**apart
    pairs = [(source, source ^ mask) for source in range(lax.axis_size(axis))]
    return lax.ppermute(value, axis, pairs)


def split_up(value, dim, count):
    shape = value.shape
    parts = value.reshape(*shape[:dim], count, shape[dim] // count, *shape[dim + 1 :])
    return jnp.moveaxis(parts, dim, 0)


def sent_and_summed(value, axis, dim):
    count = lax.axis_size(axis)
    parts = lax.all_to_all(split_up(value, dim, count), axis, 0, 0, tiled=True)
    return jnp.sum(parts, axis=0)


def copy_for_each(value, axis):
    copies = jnp.broadcast_to(value, (lax.axis_size(axis), *value.shape))
    return lax.all_to_all(copies, axis, split_axis=0, concat_axis=0, tiled=True)


def over_copies(value, axis):
    everything = copy_for_each(value, axis)
    return jnp.sum(everything, axis=0)


def unpack_mask(clip_bits, rows, width):
    shifts = jnp.arange(16, dtype=jnp.int32)
    bits = jnp.bitwise_and(jnp.right_shift(clip_bits[:, None, :], shifts[None, :, None]), 1)
    return bits.reshape(rows, width).astype(jnp.float32)


def section_terms(table, section, first, width):
    half = 1 << section
    index = first + jnp.arange(width, dtype=jnp.int32)
    pair = jnp.right_shift(index, section + 1) * half + jnp.bitwise_and(index, half - 1)
    theta = jnp.take(table[section], pair)
    lower = jnp.bitwise_and(index, half) == 0
    sign = jnp.where(lower, -1.0, 1.0).astype(jnp.float32)
    return (jnp.cos(theta), sign * jnp.sin(theta), sign, pair)


def local_partner(field, section):
    half = 1 << section
    column = jnp.arange(field.shape[1], dtype=jnp.int32)
    lower = jnp.bitwise_and(column, half) == 0
    return jnp.where(lower[None, :], jnp.roll(field, -half, axis=1), jnp.roll(field, half, axis=1))


def scatter_terms(term, pair, half_pairs):
    return jnp.zeros((half_pairs,), jnp.float32).at[pair].add(term)


def body(activations, angles, clip_bits, codes, exponents, cotangent):
    rows, width = activations.shape
    sections = angles.shape[0]
    share = angles.shape[1]
    half_pairs = share * lax.axis_size("tensor")
    local_count = width.bit_length() - 1
    place = lax.axis_index("tensor")
    table = lax.all_gather(angles, "tensor", axis=1, tiled=True)
    scale = jnp.exp2(exponents.astype(jnp.float32))
    full_cot = lax.all_gather(cotangent, "tensor", axis=1, tiled=True)
    weight_piece = (
        lax.all_gather(codes, "dp", axis=1, tiled=True).astype(jnp.float32) * scale[None, :]
    ).astype(jnp.bfloat16)
    projected = lax.dot_general(
        full_cot, weight_piece, (((1,), (1,)), ((), ())), preferred_element_type=jnp.float32
    )
    grad_rot = projected * unpack_mask(clip_bits, rows, width)
    first = place * width
    field = activations.astype(jnp.float32)
    stored = [None] * sections
    for section in range(sections):
        cosine, signed, sign, pair = section_terms(table, section, first, width)
        if section < local_count:
            other = local_partner(field, section)
        else:
            other = partner(field.astype(jnp.bfloat16), "tensor", section - local_count).astype(
                field.dtype
            )
            stored[section] = (field, other)
        field = cosine * field + signed * other
    grad = grad_rot
    terms_list = [None] * sections
    for section in reversed(range(sections)):
        cosine, signed, sign, pair = section_terms(table, section, first, width)
        if section < local_count:
            other = local_partner(field, section)
            grad_other = local_partner(grad, section)
            before = cosine * field - signed * other
        else:
            before, before_other = stored[section]
            other = cosine * before_other - signed * before
            grad_other = partner(grad, "tensor", section - local_count)
        terms_list[section] = scatter_terms(jnp.sum(sign * grad * other, axis=0), pair, half_pairs)
        grad = cosine * grad - signed * grad_other
        field = before
    input_grad = grad.astype(jnp.bfloat16)
    collected = jnp.stack(terms_list)
    partial_total = sent_and_summed(collected, "tensor", 1)
    angle_grad = over_copies(partial_total, "dp")
    return (input_grad, angle_grad)


def solution(mesh):
    placed = (
        P("dp", "tensor"),
        P(None, "tensor"),
        P("dp", "tensor"),
        P("tensor", "dp"),
        P(),
        P("dp", "tensor"),
    )
    return jax.shard_map(
        body,
        mesh=mesh,
        in_specs=placed,
        out_specs=(P("dp", "tensor"), P(None, "tensor")),
        check_vma=False,
    )
```

profile of v0, /device:TPU:1, one launch (start us, length us, event | category | flops | bytes accessed | tf_op | source)
XLA Modules:
  0.0 559.8 jit_solution(14048898341933507902)
XLA Ops:
  9.9 24.0 %all_gather.9 = f32[14,8192]{1,0:T(8,128)S(1)} all-gather(f32[14,512]{1,0:T(8,128)} %param.9), channel_id=1, replica_groups=mesh['dp'=16,'tensor'=16] {'tensor'}, dimensions={1}, use_global_device_ids=true | all-gather | bytes 487424 | tf_op jit(solution)/shard_map/all_gather | solution.py:69
  124.3 11.9 %collective-permute-done.5 = bf16[256,1024]{0,1:T(8,128)(2,1)S(1)} collective-permute-done((bf16[256,1024]{0,1:T(8,128)(2,1)}, bf16[256,1024]{0,1:T(8,128)(2,1)S(1)}, u32[]{:S(2)}, u32[]{:S(2)}) %collective-permute-start.5) | collective-permute-done | bytes 524320 | tf_op jit(solution)/shard_map/ppermute | solution.py:10
  137.7 58.5 %all-gather.3.cloned.1.call-done = bf16[1024,10240]{1,0:T(8,128)(2,1)} async-done(((bf16[1024,640]{1,0:T(8,128)(2,1)}), bf16[1024,10240]{1,0:T(8,128)(2,1)}) %all-gather.3.cloned.1.call-update) | async-done | bytes 20971536 | tf_op jit(solution)/shard_map/all_gather | solution.py:73
  196.2 12.5 %fusion.3 = f32[256,1024]{0,1:T(8,128)} fusion(bf16[256,10240]{1,0:T(8,128)(2,1)} %all-gather.5.cloned.1.call-done, bf16[1024,10240]{1,0:T(8,128)(2,1)} %all-gather.3.cloned.1.call-done, f32[10240]{0:T(1024)S(1)} %multiply_exponential_fusion, s32[256,1024]{0,1:T(8,128)} %copy.20, s32[256]{0:T(256)S(1)} %shift_right_arithmetic.224), kind=kOutput, calls=%fused_computation.32 | convolution fusion | flops 5401214976 | bytes 28353536 | tf_op jit(solution)/shard_map/dot_general | solution.py:75
  228.8 41.5 %collective-permute-done.7 = bf16[256,1024]{0,1:T(8,128)(2,1)} collective-permute-done((bf16[256,1024]{0,1:T(8,128)(2,1)}, bf16[256,1024]{0,1:T(8,128)(2,1)}, u32[]{:S(2)}, u32[]{:S(2)}) %collective-permute-start.7) | collective-permute-done | bytes 524320 | tf_op jit(solution)/shard_map/ppermute | solution.py:10
  273.1 15.1 %collective-permute-start.1 = (f32[256,1024]{0,1:T(8,128)S(1)}, f32[256,1024]{0,1:T(8,128)S(1)}, u32[]{:S(2)}, u32[]{:S(2)}) collective-permute-start(f32[256,1024]{0,1:T(8,128)S(1)} %get-tuple-element.17), channel_id=1, source_target_pairs={{0,4},{1,5},{2,6},{3,7},{4,0},{5,1},{6,2},{7,3},{8,12},{9,13},{10,... | collective-permute-start | bytes 3145736 | tf_op jit(solution)/shard_map/ppermute | solution.py:10
  288.2 46.0 %collective-permute-done.1 = f32[256,1024]{0,1:T(8,128)S(1)} collective-permute-done((f32[256,1024]{0,1:T(8,128)S(1)}, f32[256,1024]{0,1:T(8,128)S(1)}, u32[]{:S(2)}, u32[]{:S(2)}) %collective-permute-start.1) | collective-permute-done | bytes 1048608 | tf_op jit(solution)/shard_map/ppermute | solution.py:10
  336.5 22.4 %collective-permute-done.2 = f32[256,1024]{0,1:T(8,128)S(1)} collective-permute-done((f32[256,1024]{0,1:T(8,128)S(1)}, f32[256,1024]{0,1:T(8,128)S(1)}, u32[]{:S(2)}, u32[]{:S(2)}) %collective-permute-start.2) | collective-permute-done | bytes 1048608 | tf_op jit(solution)/shard_map/ppermute | solution.py:10
  364.9 7.7 %scatter_custom_fusion.13 = f32[8192]{0:T(1024)S(1)} fusion(s32[1024]{0:T(1024)S(1)} %bitcast.91, f32[1024]{0:T(1024)S(1)} %get-tuple-element.13, f32[]{:T(128)} %constant.42.clone.1), kind=kCustom, calls=%fused_computation.161 | custom fusion | flops 1024 | bytes 32772 | tf_op jit(solution)/shard_map/scatter-add | solution.py:59
  372.6 7.7 %scatter_custom_fusion.12 = f32[8192]{0:T(1024)S(1)} fusion(s32[1024]{0:T(1024)S(1)} %bitcast.89, f32[1024]{0:T(1024)S(1)} %get-tuple-element.14, f32[]{:T(128)} %constant.42.clone.1), kind=kCustom, calls=%fused_computation.163 | custom fusion | flops 1024 | bytes 32772 | tf_op jit(solution)/shard_map/scatter-add | solution.py:59
  380.3 7.7 %scatter_custom_fusion.11 = f32[8192]{0:T(1024)S(1)} fusion(s32[1024]{0:T(1024)S(1)} %bitcast.90, f32[1024]{0:T(1024)S(1)} %get-tuple-element.15, f32[]{:T(128)} %constant.42.clone.1), kind=kCustom, calls=%fused_computation.165 | custom fusion | flops 1024 | bytes 32772 | tf_op jit(solution)/shard_map/scatter-add | solution.py:59
  387.9 7.8 %scatter_custom_fusion.10 = f32[8192]{0:T(1024)S(1)} fusion(s32[1024]{0:T(1024)S(1)} %bitcast.88, f32[1024]{0:T(1024)S(1)} %get-tuple-element.16, f32[]{:T(128)} %constant.42.clone.1), kind=kCustom, calls=%fused_computation.167 | custom fusion | flops 1024 | bytes 32772 | tf_op jit(solution)/shard_map/scatter-add | solution.py:59
  425.7 7.8 %scatter_custom_fusion.9 = f32[8192]{0:T(1024)S(1)} fusion(s32[1024]{0:T(1024)} %bitcast.79, f32[1024]{0:T(1024)S(1)} %get-tuple-element.23, f32[]{:T(128)} %constant.42.clone.1), kind=kCustom, calls=%fused_computation.169 | custom fusion | flops 1024 | bytes 33280 | tf_op jit(solution)/shard_map/scatter-add | solution.py:59
  433.5 7.8 %scatter_custom_fusion.8 = f32[8192]{0:T(1024)S(1)} fusion(s32[1024]{0:T(1024)} %bitcast.87, f32[1024]{0:T(1024)S(1)} %get-tuple-element.25, f32[]{:T(128)} %constant.42.clone.1), kind=kCustom, calls=%fused_computation.171 | custom fusion | flops 1024 | bytes 33280 | tf_op jit(solution)/shard_map/scatter-add | solution.py:59
  441.3 7.8 %scatter_custom_fusion.7 = f32[8192]{0:T(1024)S(1)} fusion(s32[1024]{0:T(1024)} %bitcast.86, f32[1024]{0:T(1024)S(1)} %get-tuple-element.27, f32[]{:T(128)} %constant.42.clone.1), kind=kCustom, calls=%fused_computation.173 | custom fusion | flops 1024 | bytes 33280 | tf_op jit(solution)/shard_map/scatter-add | solution.py:59
  449.1 7.8 %scatter_custom_fusion.6 = f32[8192]{0:T(1024)S(1)} fusion(s32[1024]{0:T(1024)} %bitcast.81, f32[1024]{0:T(1024)S(1)} %get-tuple-element.29, f32[]{:T(128)} %constant.42.clone.1), kind=kCustom, calls=%fused_computation.175 | custom fusion | flops 1024 | bytes 33280 | tf_op jit(solution)/shard_map/scatter-add | solution.py:59
  456.9 7.8 %scatter_custom_fusion.5 = f32[8192]{0:T(1024)S(1)} fusion(s32[1024]{0:T(1024)} %bitcast.80, f32[1024]{0:T(1024)S(1)} %get-tuple-element.31, f32[]{:T(128)} %constant.42.clone.1), kind=kCustom, calls=%fused_computation.177 | custom fusion | flops 1024 | bytes 33280 | tf_op jit(solution)/shard_map/scatter-add | solution.py:59
  464.7 7.8 %scatter_custom_fusion.4 = f32[8192]{0:T(1024)S(1)} fusion(s32[1024]{0:T(1024)} %bitcast.83, f32[1024]{0:T(1024)S(1)} %get-tuple-element.33, f32[]{:T(128)} %constant.42.clone.1), kind=kCustom, calls=%fused_computation.179 | custom fusion | flops 1024 | bytes 33280 | tf_op jit(solution)/shard_map/scatter-add | solution.py:59
  472.5 7.8 %scatter_custom_fusion.3 = f32[8192]{0:T(1024)S(1)} fusion(s32[1024]{0:T(1024)} %bitcast.82, f32[1024]{0:T(1024)S(1)} %get-tuple-element.35, f32[]{:T(128)} %constant.42.clone.1), kind=kCustom, calls=%fused_computation.181 | custom fusion | flops 1024 | bytes 33280 | tf_op jit(solution)/shard_map/scatter-add | solution.py:59
  480.3 7.8 %scatter_custom_fusion.2 = f32[8192]{0:T(1024)S(1)} fusion(s32[1024]{0:T(1024)} %bitcast.85, f32[1024]{0:T(1024)S(1)} %get-tuple-element.37, f32[]{:T(128)} %constant.42.clone.1), kind=kCustom, calls=%fused_computation.183 | custom fusion | flops 1024 | bytes 33280 | tf_op jit(solution)/shard_map/scatter-add | solution.py:59
  488.1 8.6 %scatter_custom_fusion.1 = f32[8192]{0:T(1024)} fusion(s32[1024]{0:T(1024)} %bitcast.84, f32[1024]{0:T(1024)S(1)} %get-tuple-element.39, f32[]{:T(128)} %constant.42.clone.1), kind=kCustom, calls=%fused_computation.185 | custom fusion | flops 1024 | bytes 33280 | tf_op jit(solution)/shard_map/scatter-add | solution.py:59
  500.5 7.8 %scatter_custom_fusion = f32[8192]{0:T(1024)S(1)} fusion(s32[1024]{0:T(1024)} %bitcast.78, f32[1024]{0:T(1024)} %get-tuple-element.41, f32[]{:T(128)} %constant.42.clone.1), kind=kCustom, calls=%fused_computation.187 | custom fusion | flops 1024 | bytes 33280 | tf_op jit(solution)/shard_map/scatter-add | solution.py:59
  515.4 17.1 %all-to-all-done = f32[16,14,512]{2,1,0:T(8,128)} async-done(((f32[16,14,512]{2,1,0:T(8,128)}), f32[16,14,512]{2,1,0:T(8,128)}, u32[]{:S(2)}, u32[]{:S(2)}) %all-to-all-start) | async-done | bytes 458784 | tf_op jit(solution)/shard_map/all_to_all | solution.py:21
  544.2 6.6 %all-to-all-done.1 = f32[16,14,512]{2,1,0:T(8,128)} async-done(((f32[16,14,512]{2,1,0:T(8,128)}), f32[16,14,512]{2,1,0:T(8,128)}, u32[]{:S(2)}, u32[]{:S(2)}) %all-to-all-start.1) | async-done | bytes 458784 | tf_op jit(solution)/shard_map/all_to_all | solution.py:27
  (185 shorter events, 179.0 us)
Async XLA Ops:
  7.2 130.6 %all-gather.5.cloned.1.call-start = ((), (), s32[]{:S(2)}) async-start(), calls=%async_computation.3 | async-start | bytes 5570560 | tf_op jit(solution)/shard_map/all_gather | solution.py:71
  7.9 188.3 %all-gather.3.cloned.1.call-start = ((), (), s32[]{:S(2)}) async-start(), calls=%async_computation.2 | async-start | bytes 22282240 | tf_op jit(solution)/shard_map/all_gather | solution.py:73
  96.0 7.1 %copy-start.3 = (pred[1024]{0:T(1024)(128)(4,1)}, pred[1024]{0:T(1024)(128)(4,1)S(1)}, u32[]{:S(2)}) copy-start(pred[1024]{0:T(1024)(128)(4,1)S(1)} %and_compare_fusion) | copy-start | bytes 3076
  96.1 325.9 %copy-start.2 = (pred[1024]{0:T(1024)(128)(4,1)}, pred[1024]{0:T(1024)(128)(4,1)S(1)}, u32[]{:S(2)}) copy-start(pred[1024]{0:T(1024)(128)(4,1)S(1)} %get-tuple-element.245) | copy-start | bytes 3076
  104.2 18.6 %copy-start = (s32[16,1024]{1,0:T(8,128)S(1)}, s32[16,1024]{1,0:T(8,128)}, u32[]{:S(2)}) copy-start(s32[16,1024]{1,0:T(8,128)} %param.10) | copy-start | bytes 196612
  104.4 19.9 %copy-start.1 = (s32[10240]{0:T(1024)S(1)}, s32[10240]{0:T(1024)}, u32[]{:S(2)}) copy-start(s32[10240]{0:T(1024)} %param.12) | copy-start | bytes 122884
  108.6 13.0 %collective-permute-start.4 = (bf16[256,1024]{0,1:T(8,128)(2,1)S(1)}, bf16[256,1024]{0,1:T(8,128)(2,1)S(1)}, u32[]{:S(2)}, u32[]{:S(2)}) collective-permute-start(bf16[256,1024]{0,1:T(8,128)(2,1)S(1)} %get-tuple-element.21), channel_id=1, source_target_pairs={{0,1},{1,0},{2,3},{3,2},{4,5},{5,4},{6,7},{7,6},{8,9},{9,8},{10,11... | collective-permute-start | bytes 1572872 | tf_op jit(solution)/shard_map/ppermute | solution.py:10
  122.7 13.5 %collective-permute-start.5 = (bf16[256,1024]{0,1:T(8,128)(2,1)}, bf16[256,1024]{0,1:T(8,128)(2,1)S(1)}, u32[]{:S(2)}, u32[]{:S(2)}) collective-permute-start(bf16[256,1024]{0,1:T(8,128)(2,1)} %fusion.182), channel_id=1, source_target_pairs={{0,2},{1,3},{2,0},{3,1},{4,6},{5,7},{6,4},{7,5},{8,10},{9,11},{10,... | collective-permute-start | bytes 1572872 | tf_op jit(solution)/shard_map/ppermute | solution.py:10
  137.7 82.7 %collective-permute-start.6 = (bf16[256,1024]{0,1:T(8,128)(2,1)}, bf16[256,1024]{0,1:T(8,128)(2,1)}, u32[]{:S(2)}, u32[]{:S(2)}) collective-permute-start(bf16[256,1024]{0,1:T(8,128)(2,1)} %get-tuple-element.18), channel_id=1, source_target_pairs={{0,4},{1,5},{2,6},{3,7},{4,0},{5,1},{6,2},{7,3},{8,12},{9,13},{10,... | collective-permute-start | bytes 1572872 | tf_op jit(solution)/shard_map/ppermute | solution.py:10
  208.7 61.6 %collective-permute-start = (f32[256,1024]{0,1:T(8,128)}, f32[256,1024]{0,1:T(8,128)}, u32[]{:S(2)}, u32[]{:S(2)}) collective-permute-start(f32[256,1024]{0,1:T(8,128)} %fusion.3), channel_id=1, source_target_pairs={{0,8},{1,9},{2,10},{3,11},{4,12},{5,13},{6,14},{7,15},{8,0},{9,1},... | collective-permute-start | bytes 3145736 | tf_op jit(solution)/shard_map/ppermute | solution.py:10
  222.6 47.7 %collective-permute-start.7 = (bf16[256,1024]{0,1:T(8,128)(2,1)}, bf16[256,1024]{0,1:T(8,128)(2,1)}, u32[]{:S(2)}, u32[]{:S(2)}) collective-permute-start(bf16[256,1024]{0,1:T(8,128)(2,1)} %fusion.57), channel_id=1, source_target_pairs={{0,8},{1,9},{2,10},{3,11},{4,12},{5,13},{6,14},{7,15},{8,0},{9,1},... | collective-permute-start | bytes 1572872 | tf_op jit(solution)/shard_map/ppermute | solution.py:10
  273.1 61.2 %collective-permute-start.1 = (f32[256,1024]{0,1:T(8,128)S(1)}, f32[256,1024]{0,1:T(8,128)S(1)}, u32[]{:S(2)}, u32[]{:S(2)}) collective-permute-start(f32[256,1024]{0,1:T(8,128)S(1)} %get-tuple-element.17), channel_id=1, source_target_pairs={{0,4},{1,5},{2,6},{3,7},{4,0},{5,1},{6,2},{7,3},{8,12},{9,13},{10,... | collective-permute-start | bytes 3145736 | tf_op jit(solution)/shard_map/ppermute | solution.py:10
  334.6 24.3 %collective-permute-start.2 = (f32[256,1024]{0,1:T(8,128)S(1)}, f32[256,1024]{0,1:T(8,128)S(1)}, u32[]{:S(2)}, u32[]{:S(2)}) collective-permute-start(f32[256,1024]{0,1:T(8,128)S(1)} %multiply_subtract_fusion.11), channel_id=1, source_target_pairs={{0,2},{1,3},{2,0},{3,1},{4,6},{5,7},{6,4},{7,5},{8,10},{9,11},{10,... | collective-permute-start | bytes 3145736 | tf_op jit(solution)/shard_map/ppermute | solution.py:10
  361.0 34.8 %collective-permute-start.3 = (f32[256,1024]{0,1:T(8,128)}, f32[256,1024]{0,1:T(8,128)S(1)}, u32[]{:S(2)}, u32[]{:S(2)}) collective-permute-start(f32[256,1024]{0,1:T(8,128)} %get-tuple-element.20), channel_id=1, source_target_pairs={{0,1},{1,0},{2,3},{3,2},{4,5},{5,4},{6,7},{7,6},{8,9},{9,8},{10,11... | collective-permute-start | bytes 3145736 | tf_op jit(solution)/shard_map/ppermute | solution.py:10
  511.1 21.4 %all-to-all-start = ((f32[16,14,512]{2,1,0:T(8,128)}), f32[16,14,512]{2,1,0:T(8,128)}, u32[]{:S(2)}, u32[]{:S(2)}) async-start(f32[16,14,512]{2,1,0:T(8,128)} %bitcast.44), calls=%async_computation | async-start | bytes 1048576 | tf_op jit(solution)/shard_map/all_to_all | solution.py:21
  534.5 16.4 %all-to-all-start.1 = ((f32[16,14,512]{2,1,0:T(8,128)}), f32[16,14,512]{2,1,0:T(8,128)}, u32[]{:S(2)}, u32[]{:S(2)}) async-start(f32[16,14,512]{2,1,0:T(8,128)} %broadcast_in_dim.368), calls=%async_computation.1 | async-start | bytes 1048576 | tf_op jit(solution)/shard_map/all_to_all | solution.py:27
Sparse Core Ops, SparseCore 0:
  9.8 48.4 all-gather.4
  60.7 135.4 all-gather.2
where the time goes:
time: 569 us; the launch traced here: 560 us
  waiting for transfers between devices  205 us (36%)
  other arithmetic  167 us (29%)
  local copies, waits for them, and re-layouts  103 us (18%)
  starting transfers between devices  31.8 us (6%)
  blocking collectives  24 us (4%)
  between operations  15.6 us (3%)
  matrix products  12.5 us (2%)
    ppermute x8, waiting for transfers between devices, partner(): return lax.ppermute(value, axis, pairs)  122 us
    scatter-add x14, other arithmetic, scatter_terms(): return jnp.zeros((half_pairs,), jnp.float32).at[pair].add(term)  110 us
    gather x14, local copies, waits for them, and re-layouts, section_terms(): theta = jnp.take(table[section], pair)  86.1 us
    all_gather x1, waiting for transfers between devices, body(): lax.all_gather(codes, 'dp', axis=1, tiled=True).astype(jnp.float32)  58.5 us
    all_gather x1, blocking collectives, body(): table = lax.all_gather(angles, 'tensor', axis=1, tiled=True)  24 us
    reduce_sum x12, other arithmetic, body(): jnp.sum(sign * grad * other, axis=0)  23.8 us
    ppermute x8, starting transfers between devices, partner(): return lax.ppermute(value, axis, pairs)  22.6 us
    all_to_all x1, waiting for transfers between devices, sent_and_summed(): parts = lax.all_to_all(split_up(value, dim, count), axis, 0, 0, tiled=True)  17.1 us
  transfers between devices with their start and end apart: 12, of which 7 were waited for; matrix products, arithmetic and copies ran while one was open for 28% of the time, Pallas kernels for 0%

commit v1 on v0

v1 whole, which is shorter than its diff:
```python
import jax
import jax.numpy as jnp
from jax import lax
from jax.experimental import pallas as pl
from jax.experimental.pallas import tpu as pltpu
from jax.sharding import PartitionSpec as P

MESH = pl.DeviceIdType.MESH
F32 = jnp.float32
BF16 = jnp.bfloat16
CHUNK = 256
CHUNKS = 4


def place():
    d = lax.axis_index("dp")
    k = lax.axis_index("tensor")
    return d, k, d // 4, d % 4, k // 2, k % 2


def remote(src, dst, send, recv, to):
    return pltpu.make_async_remote_copy(
        src_ref=src, dst_ref=dst, send_sem=send, recv_sem=recv, device_id=to, device_id_type=MESH
    )


def project_kernel(
    acts, clip, codes, exps, cot, angles,
    q_out, a_out, ang_out,
    scaled, cots, w_left, w_right, w_far, sent, got, whole,
    x_send, wl_sem, wr_sem, wf_sem, b_send, b_recv, z_send, up_sem, down_sem, sib_sem,
    d_send, d_recv, e_send, e_recv, f_send, f_recv, g_send, g_recv, h_send, h_recv,
):
    d, k, x, y, z, c = place()
    slot = c * 8 + z

    def dev(px, py, pz, pc):
        return (px * 4 + py, pz * 2 + pc)

    right = dev((x + 1) % 4, y, z, c)
    left = dev((x + 3) % 4, y, z, c)
    up = dev(x, y, (z + 1) % 8, c)
    down = dev(x, y, (z + 7) % 8, c)
    sibling = dev(x, y, z, 1 - c)

    barrier = pltpu.get_barrier_semaphore()

    def greet(to):
        pl.semaphore_signal(barrier, inc=1, device_id=to, device_id_type=MESH)

    greet(right)
    greet(left)
    for step in range(1, 4):
        for core in range(2):
            greet(dev(x, (y + step) % 4, z, core))

    @pl.loop(1, 16)
    def _(i):
        greet((d, (k + i) % 16))

    pl.semaphore_wait(barrier, 23)

    for f in range(CHUNKS):
        rows = pl.ds(f * CHUNK, CHUNK)
        remote(codes.at[rows], w_left.at[rows], x_send.at[0], wl_sem.at[f], right).start()
        remote(codes.at[rows], w_right.at[rows], x_send.at[1], wr_sem.at[f], left).start()

    minus = -exps[:, pl.ds(pl.multiple_of(k * 640, 128), 640)]
    scale = jnp.ones((1, 640), F32)
    for bit in range(5):
        on = jnp.bitwise_and(jnp.right_shift(minus, bit), 1) == 1
        scale = jnp.where(on, scale * (2.0 ** -(2**bit)), scale)
    scaled[...] = (cot[...].astype(F32) * scale).astype(BF16)

    def piece(part, token_group, half):
        start = pl.multiple_of(token_group * 256 + half * 128, 128)
        return cots.at[part, pl.ds(start, 128), :]

    owner_y = k % 4
    for half in range(2):
        mine = jnp.logical_and(owner_y == y, c == half)

        @pl.when(mine)
        def _():
            start = pl.multiple_of(y * 256 + half * 128, 128)
            cots[z // 2, pl.ds(start, 128), :] = scaled[half * 128 : (half + 1) * 128, :]

        @pl.when(jnp.logical_not(mine))
        def _():
            remote(
                scaled.at[pl.ds(half * 128, 128), :],
                piece(z // 2, y, half),
                b_send.at[half],
                b_recv.at[y],
                dev(x, owner_y, z, half),
            ).start()

    ang_out[c, z, 0:14, :] = angles[...]
    ang_out[c, z, 14:16, :] = jnp.zeros((2, 512), F32)

    @pl.loop(1, 8)
    def _(i):
        remote(
            ang_out.at[c, z], ang_out.at[c, z], g_send, g_recv, (d, ((z + i) % 8) * 2 + c)
        ).start()

    def to_sibling(ref):
        remote(ref, ref, z_send.at[2], sib_sem, sibling).start()

    is_source = (z % 2) == (y // 2)

    @pl.when(is_source)
    def _():
        for g in range(4):
            ref = piece(z // 2, g, c)

            @pl.when(jnp.logical_not(jnp.logical_and(y == g, y % 2 == c)))
            def _():
                remote(ref, ref, b_send.at[0], b_recv.at[g], sibling).wait_recv()

            remote(ref, ref, z_send.at[0], up_sem.at[0, g], up).start()
            remote(ref, ref, z_send.at[1], down_sem.at[0, g], down).start()
            to_sibling(ref)

    def pass_on(t):
        below = (z + 8 - t) % 8
        above = (z + t) % 8

        @pl.when((below % 2) == (y // 2))
        def _():
            for g in range(4):
                if t < 4 or g < 2:
                    ref = piece(below // 2, g, c)
                    remote(ref, ref, z_send.at[0], up_sem.at[t - 1, g], up).wait_recv()
                    if t < 3 or (t == 3 and g < 2):
                        remote(ref, ref, z_send.at[0], up_sem.at[t, g], up).start()
                    to_sibling(ref)
                if t < 4 or g >= 2:
                    ref = piece(above // 2, g, c)
                    remote(ref, ref, z_send.at[1], down_sem.at[t - 1, g], down).wait_recv()
                    if t < 3 or (t == 3 and g >= 2):
                        remote(ref, ref, z_send.at[1], down_sem.at[t, g], down).start()
                    to_sibling(ref)

    def forward(f):
        rows = pl.ds(f * CHUNK, CHUNK)
        if f % 2 == 0:
            remote(w_left.at[rows], w_left.at[rows], x_send.at[0], wl_sem.at[f], right).wait_recv()
            remote(w_left.at[rows], w_far.at[rows], x_send.at[2], wf_sem.at[f], right).start()
        else:
            remote(w_right.at[rows], w_right.at[rows], x_send.at[1], wr_sem.at[f], left).wait_recv()
            remote(w_right.at[rows], w_far.at[rows], x_send.at[3], wf_sem.at[f], left).start()

    pass_on(1)
    pass_on(2)
    forward(0)
    forward(1)
    pass_on(3)
    pass_on(4)
    forward(2)
    forward(3)

    mine16 = pl.ds(pl.multiple_of(slot * 16, 16), 16)

    @pl.loop(1, 16)
    def _(i):
        to = (k + i) % 16
        remote(
            acts.at[pl.ds(pl.multiple_of(to * 16, 16), 16), :],
            a_out.at[mine16, :],
            f_send,
            f_recv,
            (d, to),
        ).start()

    own16 = pl.ds(pl.multiple_of(k * 16, 16), 16)
    a_out[mine16, :] = acts[own16, :]

    remote(ang_out.at[0, 0:7], ang_out.at[0, 0:7], g_send, g_recv, sibling).wait_recv()
    remote(ang_out.at[c], ang_out.at[c], h_send, h_recv, sibling).start()

    remote(cots.at[0:2], cots.at[0:2], z_send.at[2], sib_sem, sibling).wait_recv()

    def finish(f):
        lanes = pl.ds(pl.multiple_of(f * CHUNK, CHUNK), CHUNK)
        remote(got.at[f], got.at[f], d_send, d_recv.at[f], sibling).wait_recv()
        place_in_word = lax.broadcasted_iota(jnp.int32, (16, CHUNK), 0)

        def masked(w):
            rows = pl.ds(pl.multiple_of(w * 16, 16), 16)
            total = whole[f, rows, :]
            for j in range(3):
                total = total + got[f, j, rows, :].astype(F32)
            word = jnp.broadcast_to(clip[pl.ds(w, 1), lanes], (16, CHUNK))
            bit = jnp.bitwise_and(jnp.right_shift(word, place_in_word), 1)
            return rows, jnp.where(bit == 1, total, 0.0)

        @pl.loop(1, 16)
        def _(i):
            to = (k + i) % 16
            rows, value = masked(to)
            whole[f, rows, :] = value
            remote(
                whole.at[f, rows, :], q_out.at[mine16, lanes], e_send, e_recv, (d, to)
            ).start()

        _, value = masked(k)
        q_out[mine16, lanes] = value

    @pl.loop(0, 4 * CHUNKS)
    def _(i):
        f = i // 4
        j = i % 4
        to_y = (y + j + 1) % 4
        rows = pl.ds(pl.multiple_of(f * CHUNK, CHUNK), CHUNK)
        tokens = pl.ds(pl.multiple_of(to_y * 256, 256), 256)

        @pl.when(j == 0)
        def _():
            @pl.when(f % 2 == 1)
            def _():
                remote(w_left.at[rows], w_left.at[rows], x_send.at[0], wl_sem.at[f], right).wait_recv()

            @pl.when(f % 2 == 0)
            def _():
                remote(w_right.at[rows], w_right.at[rows], x_send.at[1], wr_sem.at[f], left).wait_recv()

            remote(w_far.at[rows], w_far.at[rows], x_send.at[2], wf_sem.at[f], right).wait_recv()

        def product(part, ref):
            return lax.dot_general(
                cots[part, tokens, :], ref[rows, :], (((1,), (1,)), ((), ())),
                preferred_element_type=F32,
            )

        total = product(x, codes)
        total = total + product((x + 3) % 4, w_left)
        total = total + product((x + 1) % 4, w_right)
        total = total + product((x + 2) % 4, w_far)

        @pl.when(j < 3)
        def _():
            sent[f, j] = total.astype(BF16)
            remote(
                sent.at[f, j], got.at[f, j], d_send, d_recv.at[f], dev(x, to_y, z, c)
            ).start()

        @pl.when(j == 3)
        def _():
            whole[f] = total

            @pl.when(f > 0)
            def _():
                finish(f - 1)

    finish(CHUNKS - 1)

    remote(q_out.at[0:240], q_out.at[0:240], e_send, e_recv, sibling).wait()
    remote(a_out.at[0:240], a_out.at[0:240], f_send, f_recv, sibling).wait()
    remote(ang_out.at[0, 0:7], ang_out.at[0, 0:7], g_send, g_recv, sibling).wait_send()
    remote(ang_out.at[0], ang_out.at[0], h_send, h_recv, sibling).wait()
    remote(sent, got, d_send, d_recv.at[0], sibling).wait_send()
    remote(codes, w_left, x_send.at[0], wl_sem.at[0], right).wait_send()
    remote(codes, w_right, x_send.at[1], wr_sem.at[0], left).wait_send()
    half_rows = pl.ds(0, 512)
    remote(w_left.at[half_rows], w_far.at[half_rows], x_send.at[2], wf_sem.at[0], right).wait_send()
    remote(w_left.at[half_rows], w_far.at[half_rows], x_send.at[3], wf_sem.at[0], left).wait_send()
    for half in range(2):
        @pl.when(jnp.logical_not(jnp.logical_and(owner_y == y, c == half)))
        def _():
            ref = scaled.at[pl.ds(half * 128, 128), :]
            remote(ref, ref, b_send.at[half], b_recv.at[0], sibling).wait_send()
    for way in range(2):
        @pl.when(is_source)
        def _():
            remote(cots.at[0], cots.at[0], z_send.at[way], sib_sem, sibling).wait_send()

        @pl.when(jnp.logical_not(is_source))
        def _():
            ref = cots.at[0, 0:768, :]
            remote(ref, ref, z_send.at[way], sib_sem, sibling).wait_send()
    remote(cots.at[0:2], cots.at[0:2], z_send.at[2], sib_sem, sibling).wait_send()


VMEM = pl.BlockSpec(memory_space=pltpu.VMEM)


def project(acts, clip, codes, exps, cot, angles):
    dma = pltpu.SemaphoreType.DMA
    return pl.pallas_call(
        project_kernel,
        out_shape=(
            jax.ShapeDtypeStruct((256, 1024), F32),
            jax.ShapeDtypeStruct((256, 1024), BF16),
            jax.ShapeDtypeStruct((2, 8, 16, 512), F32),
        ),
        in_specs=[VMEM] * 6,
        out_specs=(VMEM,) * 3,
        scratch_shapes=[
            pltpu.VMEM((256, 640), BF16),
            pltpu.VMEM((4, 1024, 640), BF16),
            pltpu.VMEM((1024, 640), BF16),
            pltpu.VMEM((1024, 640), BF16),
            pltpu.VMEM((1024, 640), BF16),
            pltpu.VMEM((CHUNKS, 3, 256, CHUNK), BF16),
            pltpu.VMEM((CHUNKS, 3, 256, CHUNK), BF16),
            pltpu.VMEM((CHUNKS, 256, CHUNK), F32),
            dma((4,)), dma((CHUNKS,)), dma((CHUNKS,)), dma((CHUNKS,)),
            dma((2,)), dma((4,)), dma((3,)), dma((4, 4)), dma((4, 4)), dma,
            dma, dma((CHUNKS,)), dma, dma, dma, dma, dma, dma, dma, dma,
        ],
        compiler_params=pltpu.CompilerParams(
            collective_id=0, has_side_effects=True, vmem_limit_bytes=48 * 2**20
        ),
        cost_estimate=pl.CostEstimate(flops=5400000000, bytes_accessed=6000000, transcendentals=0),
    )(acts, clip, codes, exps, cot, angles)


def sine_cosine(theta):
    h = theta * 0.5
    u = h * h
    s = 1.0 / 6227020800.0
    for term in (-1.0 / 39916800.0, 1.0 / 362880.0, -1.0 / 5040.0, 1.0 / 120.0, -1.0 / 6.0, 1.0):
        s = s * u + term
    s = s * h
    c = -1.0 / 87178291200.0
    for term in (1.0 / 479001600.0, -1.0 / 3628800.0, 1.0 / 40320.0, -1.0 / 720.0, 1.0 / 24.0, -0.5, 1.0):
        c = c * u + term
    return 2.0 * s * c, 1.0 - 2.0 * s * s


def squeezed(index, section):
    low = (1 << section) - 1
    return jnp.left_shift(jnp.right_shift(index, section + 1), section) | (index & low)


def lane_partner(value, section):
    lanes = lax.broadcasted_iota(jnp.int32, value.shape, 1)
    return jnp.take_along_axis(value, lanes ^ (1 << section), axis=1, mode="promise_in_bounds")


def pair_bit(section):
    return 8 if section == 10 else 1 << (section - 11)


def pairs_of(section):
    bit = pair_bit(section)
    pairs = []
    for m in range(8):
        b = section - 10
        lower = ((m >> b) << (b + 1)) | (m & ((1 << b) - 1))
        s0 = (lower % 2) * 8 + lower // 2
        pairs.append((m, s0, s0 + bit))
    return pairs


def butterfly_kernel(q_in, a_in, ang, q_out, g_out, cos_t, sin_t, states, terms, tall):
    lane_row = lax.broadcasted_iota(jnp.int32, (128, 128), 1)
    lane_col = lax.broadcasted_iota(jnp.int32, (128, 128), 0)
    for s in range(7):
        rows = jnp.concatenate(
            [ang[core, :, s, a * 128 : (a + 1) * 128] for a in range(4) for core in range(2)], axis=0
        )
        for b in range(2):
            pick = jnp.where(lane_col == b * 64 + squeezed(lane_row, s), 1.0, 0.0)
            theta = jnp.dot(rows, pick, precision=lax.Precision.HIGHEST, preferred_element_type=F32)
            sine, cosine = sine_cosine(theta)
            upper = (lax.broadcasted_iota(jnp.int32, theta.shape, 1) & (1 << s)) != 0
            signed = jnp.where(upper, sine, -sine)
            for a in range(4):
                cos_t[s, 2 * a + b] = cosine[a * 16 : (a + 1) * 16]
                sin_t[s, 2 * a + b] = signed[a * 16 : (a + 1) * 16]
    for s in range(7, 14):
        for a in range(4):
            for core in range(2):
                sine, cosine = sine_cosine(ang[core, :, s, a * 128 : (a + 1) * 128])
                cos_t[s, a, core * 8 : core * 8 + 8] = cosine
                sin_t[s, a, core * 8 : core * 8 + 8] = sine

    def row(table, s, tile, index):
        return jnp.broadcast_to(table[s, tile, pl.ds(index, 1), :], (16, 128))

    @pl.loop(0, 16)
    def _(kk):
        rows = pl.ds(pl.multiple_of(kk * 16, 16), 16)
        field = [a_in[rows, t * 128 : (t + 1) * 128].astype(F32) for t in range(8)]
        for s in range(7):
            for t in range(8):
                field[t] = row(cos_t, s, t, kk) * field[t] + row(sin_t, s, t, kk) * lane_partner(field[t], s)
                states[s, rows, t * 128 : (t + 1) * 128] = field[t]
        for s in range(7, 10):
            b = s - 7
            for a in range(4):
                lo = ((a >> b) << (b + 1)) | (a & ((1 << b) - 1))
                hi = lo + (1 << b)
                cosine, sine = row(cos_t, s, a, kk), row(sin_t, s, a, kk)
                field[lo], field[hi] = (
                    cosine * field[lo] - sine * field[hi],
                    sine * field[lo] + cosine * field[hi],
                )
            for t in range(8):
                states[s, rows, t * 128 : (t + 1) * 128] = field[t]

    for t in range(8):
        lanes = slice(t * 128, (t + 1) * 128)

        def fixed_row(table, s, m):
            return jnp.broadcast_to(
                table[s, t % 4, (t // 4) * 8 + m : (t // 4) * 8 + m + 1, :], (8, 128)
            )

        for s in range(10, 14):
            for m, lo, hi in pairs_of(s):
                cosine, sine = fixed_row(cos_t, s, m), fixed_row(sin_t, s, m)
                for half in range(2):
                    lo_rows = slice(lo * 16 + half * 8, lo * 16 + half * 8 + 8)
                    hi_rows = slice(hi * 16 + half * 8, hi * 16 + half * 8 + 8)
                    v_lo, v_hi = states[s - 1, lo_rows, lanes], states[s - 1, hi_rows, lanes]
                    states[s, lo_rows, lanes] = cosine * v_lo - sine * v_hi
                    states[s, hi_rows, lanes] = sine * v_lo + cosine * v_hi
        for s in (13, 12, 11, 10):
            source = q_in if s == 13 else tall
            for m, lo, hi in pairs_of(s):
                cosine, sine = fixed_row(cos_t, s, m), fixed_row(sin_t, s, m)
                total = None
                for half in range(2):
                    lo_rows = slice(lo * 16 + half * 8, lo * 16 + half * 8 + 8)
                    hi_rows = slice(hi * 16 + half * 8, hi * 16 + half * 8 + 8)
                    q_lo, q_hi = source[lo_rows, lanes], source[hi_rows, lanes]
                    term = q_hi * states[s, lo_rows, lanes] - q_lo * states[s, hi_rows, lanes]
                    total = term if total is None else total + term
                    tall[lo_rows, lanes] = cosine * q_lo + sine * q_hi
                    tall[hi_rows, lanes] = cosine * q_hi - sine * q_lo
                g_out[(t // 4) * 8 + m, s, (t % 4) * 128 : (t % 4 + 1) * 128] = jnp.sum(total, axis=0)

    @pl.loop(0, 16)
    def _(kk):
        rows = pl.ds(pl.multiple_of(kk * 16, 16), 16)
        grad = [tall[rows, t * 128 : (t + 1) * 128] for t in range(8)]
        for s in (9, 8, 7):
            b = s - 7
            for a in range(4):
                lo = ((a >> b) << (b + 1)) | (a & ((1 << b) - 1))
                hi = lo + (1 << b)
                cosine, sine = row(cos_t, s, a, kk), row(sin_t, s, a, kk)
                term = grad[hi] * states[s, rows, lo * 128 : (lo + 1) * 128]
                term = term - grad[lo] * states[s, rows, hi * 128 : (hi + 1) * 128]
                g_out[kk, s, a * 128 : (a + 1) * 128] = jnp.sum(term, axis=0)
                grad[lo], grad[hi] = (
                    cosine * grad[lo] + sine * grad[hi],
                    cosine * grad[hi] - sine * grad[lo],
                )
        for s in (6, 5, 4, 3, 2, 1, 0):
            for t in range(8):
                other = lane_partner(grad[t], s)
                term = other * states[s, rows, t * 128 : (t + 1) * 128]
                terms[s, t, pl.ds(kk, 1), :] = jnp.sum(term, axis=0, keepdims=True)
                grad[t] = row(cos_t, s, t, kk) * grad[t] - row(sin_t, s, t, kk) * other
        for t in range(8):
            q_out[rows, t * 128 : (t + 1) * 128] = grad[t].astype(BF16)

    for s in range(7):
        sign = jnp.where((lane_col & (1 << s)) == 0, 1.0, -1.0)
        for a in range(4):
            total = None
            for b in range(2):
                pick = jnp.where(lane_row == b * 64 + squeezed(lane_col, s), sign, 0.0)
                part = jnp.dot(
                    terms[s, 2 * a + b], pick, precision=lax.Precision.HIGHEST, preferred_element_type=F32
                )
                total = part if total is None else total + part
            g_out[:, s, a * 128 : (a + 1) * 128] = total
    g_out[:, 14:16, :] = jnp.zeros((16, 2, 512), F32)


def butterfly(grad, acts, ang):
    return pl.pallas_call(
        butterfly_kernel,
        out_shape=(
            jax.ShapeDtypeStruct((256, 1024), BF16),
            jax.ShapeDtypeStruct((16, 16, 512), F32),
        ),
        in_specs=[VMEM] * 3,
        out_specs=(VMEM,) * 2,
        scratch_shapes=[
            pltpu.VMEM((14, 8, 16, 128), F32),
            pltpu.VMEM((14, 8, 16, 128), F32),
            pltpu.VMEM((14, 256, 1024), F32),
            pltpu.VMEM((7, 8, 16, 128), F32),
            pltpu.VMEM((256, 1024), F32),
        ],
        compiler_params=pltpu.CompilerParams(vmem_limit_bytes=48 * 2**20),
    )(grad, acts, ang)


def return_kernel(
    grad, parts, out, angle_out, by_width, summed, by_tokens,
    a_send, a_recv, b_send, b_recv, c_send, c_recv,
):
    d, k, x, y, z, c = place()
    slot = c * 8 + z
    barrier = pltpu.get_barrier_semaphore()

    @pl.loop(1, 16)
    def _(i):
        pl.semaphore_signal(barrier, inc=1, device_id=(d, (k + i) % 16), device_id_type=MESH)
        pl.semaphore_signal(barrier, inc=1, device_id=((d + i) % 16, k), device_id_type=MESH)

    pl.semaphore_wait(barrier, 30)

    @pl.loop(1, 16)
    def _(i):
        to = (k + i) % 16
        to_slot = (to % 2) * 8 + to // 2
        remote(parts.at[to_slot], by_width.at[slot], b_send, b_recv, (d, to)).start()

    own_rows = pl.ds(pl.multiple_of(slot * 16, 16), 16)
    own_tokens = pl.ds(pl.multiple_of(k * 16, 16), 16)

    @pl.loop(1, 16)
    def _(i):
        to = (k + i) % 16
        to_slot = (to % 2) * 8 + to // 2
        rows = pl.ds(pl.multiple_of(to_slot * 16, 16), 16)
        remote(grad.at[rows, :], out.at[own_tokens, :], a_send, a_recv, (d, to)).start()

    out[own_tokens, :] = grad[own_rows, :]
    by_width[slot] = parts[slot]
    remote(by_width.at[0:15], by_width.at[0:15], b_send, b_recv, (d, (k + 1) % 16)).wait_recv()
    total = by_width[0]
    for i in range(1, 16):
        total = total + by_width[i]
    summed[...] = total
    by_tokens[d] = total

    @pl.loop(1, 16)
    def _(i):
        remote(summed, by_tokens.at[d], c_send, c_recv, ((d + i) % 16, k)).start()

    remote(by_tokens.at[0:15], by_tokens.at[0:15], c_send, c_recv, ((d + 1) % 16, k)).wait()
    total = by_tokens[0, 0:14, :]
    for i in range(1, 16):
        total = total + by_tokens[i, 0:14, :]
    angle_out[...] = total
    remote(by_width.at[0:15], by_width.at[0:15], b_send, b_recv, (d, (k + 1) % 16)).wait_send()
    remote(grad.at[0:240], out.at[0:240], a_send, a_recv, (d, (k + 1) % 16)).wait()


def give_back(grad, parts):
    dma = pltpu.SemaphoreType.DMA
    return pl.pallas_call(
        return_kernel,
        out_shape=(
            jax.ShapeDtypeStruct((256, 1024), BF16),
            jax.ShapeDtypeStruct((14, 512), F32),
        ),
        in_specs=[VMEM] * 2,
        out_specs=(VMEM,) * 2,
        scratch_shapes=[
            pltpu.VMEM((16, 16, 512), F32),
            pltpu.VMEM((16, 512), F32),
            pltpu.VMEM((16, 16, 512), F32),
            dma, dma, dma, dma, dma, dma,
        ],
        compiler_params=pltpu.CompilerParams(
            collective_id=1, has_side_effects=True, vmem_limit_bytes=32 * 2**20
        ),
    )(grad, parts)


def body(activations, angles, clip_bits, codes, exponents, cotangent):
    grad, acts, ang = project(
        activations, clip_bits, codes, exponents[None, :], cotangent, angles
    )
    grad, parts = butterfly(grad, acts, ang)
    return give_back(grad, parts)


def solution(mesh):
    placed = (
        P("dp", "tensor"),
        P(None, "tensor"),
        P("dp", "tensor"),
        P("tensor", "dp"),
        P(),
        P("dp", "tensor"),
    )
    return jax.shard_map(
        body,
        mesh=mesh,
        in_specs=placed,
        out_specs=(P("dp", "tensor"), P(None, "tensor")),
        check_vma=False,
    )
```

time: 569 us -> 151 us (0.27); the launches traced: 560 us -> 151 us
  waiting for transfers between devices: 205 us -> 0 us
  other arithmetic: 167 us -> 0 us
  Pallas kernels: 0 us -> 143 us
  local copies, waits for them, and re-layouts: 103 us -> 7.11 us
  starting transfers between devices: 31.8 us -> 0 us
  blocking collectives: 24 us -> 0 us
  between operations: 15.6 us -> 0.67 us
  matrix products: 12.5 us -> 0 us
    pallas_call x0 -> x3, Pallas kernels: none -> 143 us  [the longest x1 87.8 us: project(): pl.pallas_call(project_kernel, out_shape=(jax.ShapeDtypeStruct((256, 1024...]
    ppermute x8 -> x0, waiting for transfers between devices: 122 us -> none  [partner(): return lax.ppermute(value, axis, pairs)]
    scatter-add x14 -> x0, other arithmetic: 110 us -> none  [scatter_terms(): return jnp.zeros((half_pairs,), jnp.float32).at[pair].add(term)]
    gather x14 -> x0, local copies, waits for them, and re-layouts: 86.1 us -> none  [section_terms(): theta = jnp.take(table[section], pair)]
    all_gather x2 -> x0, waiting for transfers between devices: 58.5 us -> none  [the longest x1 58.5 us: body(): lax.all_gather(codes, 'dp', axis=1, tiled=True).astype(jnp.float32)]
    reduce_sum x14 -> x0, other arithmetic: 26.6 us -> none  [the longest x12 23.8 us: body(): jnp.sum(sign * grad * other, axis=0)]
    all_gather x1 -> x0, blocking collectives: 24 us -> none  [body(): table = lax.all_gather(angles, 'tensor', axis=1, tiled=True)]
    all_to_all x2 -> x0, waiting for transfers between devices: 23.7 us -> none  [the longest x1 17.1 us: sent_and_summed(): parts = lax.all_to_all(split_up(value, dim, count), axis, 0, 0, tiled=True)]
  transfers between devices with their start and end apart: 12 -> 0, of which waited for: 7 -> 0; matrix products, arithmetic and copies ran while one was open for 28% -> 0% of each run, Pallas kernels for 0% -> 0%
where the time goes in v1:
time: 151 us
  Pallas kernels  143 us (95%)
  local copies, waits for them, and re-layouts  7.11 us (5%)
    pallas_call x1, Pallas kernels, project(): pl.pallas_call(project_kernel, out_shape=(jax.ShapeDtypeStruct((256, 1024...  87.8 us
    pallas_call x1, Pallas kernels, give_back(): pl.pallas_call(return_kernel, out_shape=(jax.ShapeDtypeStruct((256, 1024)...  30.2 us
    pallas_call x1, Pallas kernels, butterfly(): pl.pallas_call(butterfly_kernel, out_shape=(jax.ShapeDtypeStruct((256, 10...  25 us
    unnamed x14, local copies, waits for them, and re-layouts  7.11 us

profile of v1, /device:TPU:1, one launch (start us, length us, event | category | flops | bytes accessed | tf_op | source)
XLA Modules:
  0.0 150.7 jit_solution(17023313767292219664)
XLA Ops:
  0.6 0.0 copy-start
  0.6 1.3 copy-done
  1.9 0.0 copy-start.1
  2.0 1.0 copy-done.1
  3.0 0.0 copy-start.2
  3.0 1.0 copy-done.2
  4.0 0.0 copy-start.3
  4.0 0.8 copy-done.3
  4.8 0.0 copy-start.4
  4.8 0.8 copy-done.4
  5.6 0.0 copy-start.5
  5.6 0.8 copy-done.5
  6.3 87.8 %shard_map.77 = (f32[256,1024]{1,0:T(8,128)S(1)}, bf16[256,1024]{1,0:T(8,128)(2,1)S(1)}, f32[2,8,16,512]{3,2,1,0:T(8,128)S(1)}) custom-call(bf16[256,1024]{1,0:T(8,128)(2,1)S(1)} %copy-done.1, s32[16,1024]{1,0:T(8,128)S(1)} %copy-done.3, bf16[1024,640]{1,0:T(8,128)(2,1)S(1)} %copy-done, s32[1,10240]{1,0:T(1,128)S(1)} %bitcast.1, ...), custom_call_target="tpu_custom_call" | custom-call | flops 5400000000 | bytes 6000000 | tf_op jit(solution)/shard_map/pallas_call | solution.py:290
  94.1 25.0 %shard_map.78 = (bf16[256,1024]{1,0:T(8,128)(2,1)S(1)}, f32[16,16,512]{2,1,0:T(8,128)S(1)}) custom-call(f32[256,1024]{1,0:T(8,128)S(1)} %get-tuple-element.7.q_in, bf16[256,1024]{1,0:T(8,128)(2,1)S(1)} %get-tuple-element.8.a_in, f32[2,8,16,512]{3,2,1,0:T(8,128)S(1)} %get-tuple-element.9.ang), custom_call_target="tpu_custom_call" | custom-call | tf_op jit(solution)/shard_map/pallas_call | solution.py:477
  119.1 30.2 %shard_map.79 = (bf16[256,1024]{1,0:T(8,128)(2,1)S(1)}, f32[14,512]{1,0:T(8,128)S(1)}) custom-call(bf16[256,1024]{1,0:T(8,128)(2,1)S(1)} %get-tuple-element.10.grad, f32[16,16,512]{2,1,0:T(8,128)S(1)} %get-tuple-element.11.parts), custom_call_target="tpu_custom_call" | custom-call | tf_op jit(solution)/shard_map/pallas_call | solution.py:551
  149.3 0.8 copy.10
  150.1 0.6 copy.11
Async XLA Ops:
  0.6 1.3 copy-start
  1.9 1.0 copy-start.1
  3.0 1.0 copy-start.2
  4.0 0.8 copy-start.3
  4.8 0.8 copy-start.4
  5.6 0.8 copy-start.5

commit v2 on v1

v2 whole, which is shorter than its diff:
```python
import jax
import jax.numpy as jnp
from jax import lax
from jax.experimental import pallas as pl
from jax.experimental.pallas import tpu as pltpu
from jax.sharding import PartitionSpec as P

MESH = pl.DeviceIdType.MESH
F32 = jnp.float32
BF16 = jnp.bfloat16
CHUNK = 256
CHUNKS = 4


def place():
    d = lax.axis_index("dp")
    k = lax.axis_index("tensor")
    return d, k, d // 4, d % 4, k // 2, k % 2


def remote(src, dst, send, recv, to):
    return pltpu.make_async_remote_copy(
        src_ref=src, dst_ref=dst, send_sem=send, recv_sem=recv, device_id=to, device_id_type=MESH
    )


def sine_cosine(theta):
    h = theta * 0.5
    u = h * h
    s = 1.0 / 6227020800.0
    for term in (-1.0 / 39916800.0, 1.0 / 362880.0, -1.0 / 5040.0, 1.0 / 120.0, -1.0 / 6.0, 1.0):
        s = s * u + term
    s = s * h
    c = -1.0 / 87178291200.0
    for term in (1.0 / 479001600.0, -1.0 / 3628800.0, 1.0 / 40320.0, -1.0 / 720.0, 1.0 / 24.0, -0.5, 1.0):
        c = c * u + term
    return 2.0 * s * c, 1.0 - 2.0 * s * s


def squeezed(index, section):
    low = (1 << section) - 1
    return jnp.left_shift(jnp.right_shift(index, section + 1), section) | (index & low)


def lane_partner(value, section):
    lanes = lax.broadcasted_iota(jnp.int32, value.shape, 1)
    return jnp.take_along_axis(value, lanes ^ (1 << section), axis=1, mode="promise_in_bounds")


def pair_bit(section):
    return 8 if section == 10 else 1 << (section - 11)


def pairs_of(section):
    bit = pair_bit(section)
    pairs = []
    for m in range(8):
        b = section - 10
        lower = ((m >> b) << (b + 1)) | (m & ((1 << b) - 1))
        s0 = (lower % 2) * 8 + lower // 2
        pairs.append((m, s0, s0 + bit))
    return pairs


def all_kernel(
    acts, clip, codes, exps, cot, angles,
    out, angle_out,
    clip_v, exps_v, cot_v, ang_v, w_own,
    scaled, cots, w_left, w_right, w_far, sent, got, whole,
    q_in, a_in, ang, cos_t, sin_t, states, terms, tops, tall, q_back,
    parts, by_tokens, row_out, by_width, final,
    l_sem, x_send, wl_sem, wr_sem, wf_sem, b_send, b_recv, z_send, up_sem, down_sem, sib_sem,
    d_send, d_recv, e_send, e_recv, f_send, f_recv, g_send, g_recv, h_send, h_recv,
    o_send, o_recv, p_send, p_recv, r_send, r_recv, t_send, t_recv,
):
    d, k, x, y, z, c = place()
    slot = c * 8 + z
    mine16 = pl.ds(pl.multiple_of(slot * 16, 16), 16)
    own16 = pl.ds(pl.multiple_of(k * 16, 16), 16)

    def dev(px, py, pz, pc):
        return (px * 4 + py, pz * 2 + pc)

    right = dev((x + 1) % 4, y, z, c)
    left = dev((x + 3) % 4, y, z, c)
    up = dev(x, y, (z + 1) % 8, c)
    down = dev(x, y, (z + 7) % 8, c)
    sibling = dev(x, y, z, 1 - c)

    loads = [
        pltpu.make_async_copy(cot, cot_v, l_sem.at[0]),
        pltpu.make_async_copy(exps.at[:, pl.ds(pl.multiple_of(k * 640, 128), 640)], exps_v, l_sem.at[1]),
        pltpu.make_async_copy(angles, ang_v, l_sem.at[2]),
        pltpu.make_async_copy(codes, w_own, l_sem.at[3]),
        pltpu.make_async_copy(clip, clip_v, l_sem.at[4]),
    ]
    own_copy = pltpu.make_async_copy(acts.at[own16, :], a_in.at[mine16, :], l_sem.at[5])
    barrier = pltpu.get_barrier_semaphore()

    def greet(to):
        pl.semaphore_signal(barrier, inc=1, device_id=to, device_id_type=MESH)

    for copy in loads:
        copy.start()
    own_copy.start()

    @pl.loop(1, 16)
    def _(i):
        greet((d, (k + i) % 16))
        greet(((d + i) % 16, k))

    for step in range(1, 4):
        greet(dev(x, (y + step) % 4, z, 1 - c))
    pl.semaphore_wait(barrier, 33)

    def send_activations():
        @pl.loop(1, 16)
        def _(i):
            to = (k + i) % 16
            remote(
                acts.at[pl.ds(pl.multiple_of(to * 16, 16), 16), :], a_in.at[mine16, :], f_send, f_recv, (d, to)
            ).start()

    for f in range(CHUNKS):
        rows = pl.ds(f * CHUNK, CHUNK)
        remote(codes.at[rows], w_left.at[rows], x_send.at[0], wl_sem.at[f], right).start()
        remote(codes.at[rows], w_right.at[rows], x_send.at[1], wr_sem.at[f], left).start()

    for n in range(3):
        loads[n].wait()
    minus = -exps_v[...]
    scale = jnp.ones((1, 640), F32)
    for bit in range(5):
        on = jnp.bitwise_and(jnp.right_shift(minus, bit), 1) == 1
        scale = jnp.where(on, scale * (2.0 ** -(2**bit)), scale)
    scaled[...] = (cot_v[...].astype(F32) * scale).astype(BF16)

    def piece(part, token_group, half):
        start = pl.multiple_of(token_group * 256 + half * 128, 128)
        return cots.at[part, pl.ds(start, 128), :]

    owner_y = k % 4
    for half in range(2):
        mine = jnp.logical_and(owner_y == y, c == half)

        @pl.when(mine)
        def _():
            start = pl.multiple_of(y * 256 + half * 128, 128)
            cots[z // 2, pl.ds(start, 128), :] = scaled[half * 128 : (half + 1) * 128, :]

        @pl.when(jnp.logical_not(mine))
        def _():
            remote(
                scaled.at[pl.ds(half * 128, 128), :],
                piece(z // 2, y, half),
                b_send.at[half],
                b_recv.at[y],
                dev(x, owner_y, z, half),
            ).start()

    ang[c, z, 0:14, :] = ang_v[...]
    ang[c, z, 14:16, :] = jnp.zeros((2, 512), F32)

    @pl.loop(1, 8)
    def _(i):
        remote(
            ang.at[c, z], ang.at[c, z], g_send, g_recv, (d, ((z + i) % 8) * 2 + c)
        ).start()

    def to_sibling(ref):
        remote(ref, ref, z_send.at[2], sib_sem, sibling).start()

    is_source = (z % 2) == (y // 2)

    @pl.when(is_source)
    def _():
        for g in range(4):
            ref = piece(z // 2, g, c)

            @pl.when(jnp.logical_not(jnp.logical_and(y == g, y % 2 == c)))
            def _():
                remote(ref, ref, b_send.at[0], b_recv.at[g], sibling).wait_recv()

            remote(ref, ref, z_send.at[0], up_sem.at[0, g], up).start()
            remote(ref, ref, z_send.at[1], down_sem.at[0, g], down).start()
            to_sibling(ref)

    def pass_on(t):
        below = (z + 8 - t) % 8
        above = (z + t) % 8

        @pl.when((below % 2) == (y // 2))
        def _():
            for g in range(4):
                if t < 4 or g < 2:
                    ref = piece(below // 2, g, c)
                    remote(ref, ref, z_send.at[0], up_sem.at[t - 1, g], up).wait_recv()
                    if t < 3 or (t == 3 and g < 2):
                        remote(ref, ref, z_send.at[0], up_sem.at[t, g], up).start()
                    to_sibling(ref)
                if t < 4 or g >= 2:
                    ref = piece(above // 2, g, c)
                    remote(ref, ref, z_send.at[1], down_sem.at[t - 1, g], down).wait_recv()
                    if t < 3 or (t == 3 and g >= 2):
                        remote(ref, ref, z_send.at[1], down_sem.at[t, g], down).start()
                    to_sibling(ref)

    def forward(f):
        rows = pl.ds(f * CHUNK, CHUNK)
        if f % 2 == 0:
            remote(w_left.at[rows], w_left.at[rows], x_send.at[0], wl_sem.at[f], right).wait_recv()
            remote(w_left.at[rows], w_far.at[rows], x_send.at[2], wf_sem.at[f], right).start()
        else:
            remote(w_right.at[rows], w_right.at[rows], x_send.at[1], wr_sem.at[f], left).wait_recv()
            remote(w_right.at[rows], w_far.at[rows], x_send.at[3], wf_sem.at[f], left).start()

    pass_on(1)
    pass_on(2)
    forward(0)
    forward(1)
    pass_on(3)
    send_activations()

    remote(ang.at[0, 0:7], ang.at[0, 0:7], g_send, g_recv, sibling).wait_recv()
    remote(ang.at[c], ang.at[c], h_send, h_recv, sibling).start()
    forward(2)
    forward(3)
    pass_on(4)
    remote(ang.at[0], ang.at[0], h_send, h_recv, sibling).wait_recv()
    lane_row = lax.broadcasted_iota(jnp.int32, (128, 128), 1)
    lane_col = lax.broadcasted_iota(jnp.int32, (128, 128), 0)
    for s in range(7):
        rows = jnp.concatenate(
            [ang[core, :, s, a * 128 : (a + 1) * 128] for a in range(4) for core in range(2)], axis=0
        )
        for b in range(2):
            pick = jnp.where(lane_col == b * 64 + squeezed(lane_row, s), 1.0, 0.0)
            theta = jnp.dot(rows, pick, precision=lax.Precision.HIGHEST, preferred_element_type=F32)
            sine, cosine = sine_cosine(theta)
            upper = (lax.broadcasted_iota(jnp.int32, theta.shape, 1) & (1 << s)) != 0
            signed = jnp.where(upper, sine, -sine)
            for a in range(4):
                cos_t[s, 2 * a + b] = cosine[a * 16 : (a + 1) * 16]
                sin_t[s, 2 * a + b] = signed[a * 16 : (a + 1) * 16]
    for s in range(7, 14):
        for a in range(4):
            for core in range(2):
                sine, cosine = sine_cosine(ang[core, :, s, a * 128 : (a + 1) * 128])
                cos_t[s, a, core * 8 : core * 8 + 8] = cosine
                sin_t[s, a, core * 8 : core * 8 + 8] = sine


    remote(cots.at[0:2], cots.at[0:2], z_send.at[2], sib_sem, sibling).wait_recv()

    def finish(f):
        lanes = pl.ds(pl.multiple_of(f * CHUNK, CHUNK), CHUNK)
        remote(got.at[f], got.at[f], d_send, d_recv.at[f], sibling).wait_recv()
        place_in_word = lax.broadcasted_iota(jnp.int32, (16, CHUNK), 0)

        def masked(w):
            rows = pl.ds(pl.multiple_of(w * 16, 16), 16)
            total = whole[f, rows, :]
            for j in range(3):
                total = total + got[f, j, rows, :].astype(F32)
            word = jnp.broadcast_to(clip_v[pl.ds(w, 1), lanes], (16, CHUNK))
            bit = jnp.bitwise_and(jnp.right_shift(word, place_in_word), 1)
            return rows, jnp.where(bit == 1, total, 0.0)

        @pl.loop(1, 16)
        def _(i):
            to = (k + i) % 16
            rows, value = masked(to)
            whole[f, rows, :] = value
            remote(
                whole.at[f, rows, :], q_in.at[mine16, lanes], e_send, e_recv, (d, to)
            ).start()

        _, value = masked(k)
        q_in[mine16, lanes] = value

    loads[3].wait()
    loads[4].wait()
    own_copy.wait()

    @pl.loop(0, 4 * CHUNKS)
    def _(i):
        f = i // 4
        j = i % 4
        to_y = (y + j + 1) % 4
        rows = pl.ds(pl.multiple_of(f * CHUNK, CHUNK), CHUNK)
        tokens = pl.ds(pl.multiple_of(to_y * 256, 256), 256)

        @pl.when(j == 0)
        def _():
            @pl.when(f % 2 == 1)
            def _():
                remote(w_left.at[rows], w_left.at[rows], x_send.at[0], wl_sem.at[f], right).wait_recv()

            @pl.when(f % 2 == 0)
            def _():
                remote(w_right.at[rows], w_right.at[rows], x_send.at[1], wr_sem.at[f], left).wait_recv()

            remote(w_far.at[rows], w_far.at[rows], x_send.at[2], wf_sem.at[f], right).wait_recv()

        def product(part, ref):
            return lax.dot_general(
                cots[part, tokens, :], ref[rows, :], (((1,), (1,)), ((), ())),
                preferred_element_type=F32,
            )

        total = product(x, w_own)
        total = total + product((x + 3) % 4, w_left)
        total = total + product((x + 1) % 4, w_right)
        total = total + product((x + 2) % 4, w_far)

        @pl.when(j < 3)
        def _():
            sent[f, j] = total.astype(BF16)
            remote(
                sent.at[f, j], got.at[f, j], d_send, d_recv.at[f], dev(x, to_y, z, c)
            ).start()

        @pl.when(j == 3)
        def _():
            whole[f] = total

            @pl.when(f > 0)
            def _():
                finish(f - 1)

    finish(CHUNKS - 1)

    remote(a_in.at[0:240], a_in.at[0:240], f_send, f_recv, sibling).wait()

    def row(table, s, tile, index):
        return jnp.broadcast_to(table[s, tile, pl.ds(index, 1), :], (16, 128))

    @pl.loop(0, 16)
    def _(kk):
        rows = pl.ds(pl.multiple_of(kk * 16, 16), 16)
        field = [a_in[rows, t * 128 : (t + 1) * 128].astype(F32) for t in range(8)]
        for s in range(7):
            for t in range(8):
                field[t] = row(cos_t, s, t, kk) * field[t] + row(sin_t, s, t, kk) * lane_partner(field[t], s)
                states[s, rows, t * 128 : (t + 1) * 128] = field[t]
        for s in range(7, 10):
            b = s - 7
            for a in range(4):
                lo = ((a >> b) << (b + 1)) | (a & ((1 << b) - 1))
                hi = lo + (1 << b)
                cosine, sine = row(cos_t, s, a, kk), row(sin_t, s, a, kk)
                field[lo], field[hi] = (
                    cosine * field[lo] - sine * field[hi],
                    sine * field[lo] + cosine * field[hi],
                )
            for t in range(8):
                states[s, rows, t * 128 : (t + 1) * 128] = field[t]

    def fixed_row(table, s, t, m):
        return jnp.broadcast_to(table[s, t % 4, pl.ds((t // 4) * 8 + m, 1), :], (8, 128))

    def halves(lo, hi):
        for half in range(2):
            yield slice(lo * 16 + half * 8, lo * 16 + half * 8 + 8), slice(hi * 16 + half * 8, hi * 16 + half * 8 + 8)

    @pl.loop(0, 8)
    def _(t):
        lanes = pl.ds(pl.multiple_of(t * 128, 128), 128)
        for s in range(10, 14):
            for m, lo, hi in pairs_of(s):
                cosine, sine = fixed_row(cos_t, s, t, m), fixed_row(sin_t, s, t, m)
                for lo_rows, hi_rows in halves(lo, hi):
                    v_lo, v_hi = states[s - 1, lo_rows, lanes], states[s - 1, hi_rows, lanes]
                    states[s, lo_rows, lanes] = cosine * v_lo - sine * v_hi
                    states[s, hi_rows, lanes] = sine * v_lo + cosine * v_hi

    remote(q_in.at[0:240], q_in.at[0:240], e_send, e_recv, sibling).wait()

    def to_section_owner(s):
        @pl.when(d != s)
        def _():
            remote(parts.at[s], by_tokens.at[d], p_send, p_recv, (s, k)).start()

        @pl.when(d == s)
        def _():
            by_tokens[d] = parts[s]

    @pl.loop(0, 8)
    def _(t):
        lanes = pl.ds(pl.multiple_of(t * 128, 128), 128)
        for s in (13, 12, 11, 10):
            source = q_in if s == 13 else tall
            for m, lo, hi in pairs_of(s):
                cosine, sine = fixed_row(cos_t, s, t, m), fixed_row(sin_t, s, t, m)
                total = None
                for lo_rows, hi_rows in halves(lo, hi):
                    q_lo, q_hi = source[lo_rows, lanes], source[hi_rows, lanes]
                    term = q_hi * states[s, lo_rows, lanes] - q_lo * states[s, hi_rows, lanes]
                    total = term if total is None else total + term
                    tall[lo_rows, lanes] = cosine * q_lo + sine * q_hi
                    tall[hi_rows, lanes] = cosine * q_hi - sine * q_lo
                tops[s - 7, t % 4, pl.ds((t // 4) * 8 + m, 1), :] = jnp.sum(total, axis=0, keepdims=True)

    def laid_out(first, last):
        for s in range(first, last):
            for a in range(4):
                parts[s, :, a * 128 : (a + 1) * 128] = tops[s - 7, a]

    laid_out(10, 14)

    @pl.loop(0, 4)
    def _(i):
        to_section_owner(10 + (d + i) % 4)

    @pl.loop(0, 16)
    def _(i):
        kk = (slot + 1 + i) % 16
        rows = pl.ds(pl.multiple_of(kk * 16, 16), 16)
        grad = [tall[rows, t * 128 : (t + 1) * 128] for t in range(8)]
        for s in (9, 8, 7):
            b = s - 7
            for a in range(4):
                lo = ((a >> b) << (b + 1)) | (a & ((1 << b) - 1))
                hi = lo + (1 << b)
                cosine, sine = row(cos_t, s, a, kk), row(sin_t, s, a, kk)
                term = grad[hi] * states[s, rows, lo * 128 : (lo + 1) * 128]
                term = term - grad[lo] * states[s, rows, hi * 128 : (hi + 1) * 128]
                tops[s - 7, a, pl.ds(kk, 1), :] = jnp.sum(term, axis=0, keepdims=True)
                grad[lo], grad[hi] = (
                    cosine * grad[lo] + sine * grad[hi],
                    cosine * grad[hi] - sine * grad[lo],
                )
        for s in (6, 5, 4, 3, 2, 1, 0):
            for t in range(8):
                other = lane_partner(grad[t], s)
                term = other * states[s, rows, t * 128 : (t + 1) * 128]
                terms[s, t, pl.ds(kk, 1), :] = jnp.sum(term, axis=0, keepdims=True)
                grad[t] = row(cos_t, s, t, kk) * grad[t] - row(sin_t, s, t, kk) * other
        for t in range(8):
            q_back[rows, t * 128 : (t + 1) * 128] = grad[t].astype(BF16)

        @pl.when(i < 15)
        def _():
            to = (kk % 8) * 2 + kk // 8
            remote(q_back.at[rows, :], out.at[own16, :], o_send, o_recv, (d, to)).start()

        @pl.when(i == 15)
        def _():
            out[own16, :] = q_back[rows, :]

    laid_out(7, 10)
    for s in range(7):
        sign = jnp.where((lane_col & (1 << s)) == 0, 1.0, -1.0)
        total = None
        for b in range(2):
            pick = jnp.where(lane_row == b * 64 + squeezed(lane_col, s), sign, 0.0)
            rows = jnp.concatenate([terms[s, 2 * a + b] for a in range(4)], axis=0)
            part = jnp.dot(rows, pick, precision=lax.Precision.HIGHEST, preferred_element_type=F32)
            total = part if total is None else total + part
        for a in range(4):
            parts[s, :, a * 128 : (a + 1) * 128] = total[a * 16 : (a + 1) * 16]

    @pl.loop(0, 10)
    def _(i):
        to_section_owner((d + i) % 10)

    @pl.when(d < 14)
    def _():
        remote(by_tokens.at[0:15], by_tokens.at[0:15], p_send, p_recv, sibling).wait_recv()
        total = by_tokens[0]
        for i in range(1, 16):
            total = total + by_tokens[i]
        for j in range(16):
            row_out[j] = total[j : j + 1, :]

        @pl.loop(1, 16)
        def _(i):
            other = (slot + i) % 16
            remote(
                row_out.at[other], by_width.at[slot], r_send, r_recv, (d, (other % 8) * 2 + other // 8)
            ).start()

        by_width[slot] = row_out[slot]
        remote(by_width.at[0:15], by_width.at[0:15], r_send, r_recv, sibling).wait_recv()
        total = by_width[0]
        for i in range(1, 16):
            total = total + by_width[i]
        final[d] = total

        @pl.loop(1, 16)
        def _(i):
            remote(final.at[d], final.at[d], t_send, t_recv, ((d + i) % 16, k)).start()

        remote(final.at[0:13], final.at[0:13], t_send, t_recv, sibling).wait_recv()
        remote(by_tokens.at[0:13], by_tokens.at[0:13], p_send, p_recv, sibling).wait_send()
        remote(by_width.at[0:15], by_width.at[0:15], r_send, r_recv, sibling).wait_send()
        remote(final.at[0:15], final.at[0:15], t_send, t_recv, sibling).wait_send()

    @pl.when(d >= 14)
    def _():
        remote(final.at[0:14], final.at[0:14], t_send, t_recv, sibling).wait_recv()
        remote(by_tokens.at[0:14], by_tokens.at[0:14], p_send, p_recv, sibling).wait_send()

    for s in range(14):
        angle_out[s : s + 1, :] = final[s]

    remote(q_back.at[0:240], out.at[0:240], o_send, o_recv, sibling).wait()
    remote(ang.at[0, 0:7], ang.at[0, 0:7], g_send, g_recv, sibling).wait_send()
    remote(ang.at[0], ang.at[0], h_send, h_recv, sibling).wait_send()
    remote(sent, got, d_send, d_recv.at[0], sibling).wait_send()
    remote(w_own, w_left, x_send.at[0], wl_sem.at[0], right).wait_send()
    remote(w_own, w_right, x_send.at[1], wr_sem.at[0], left).wait_send()
    half_rows = pl.ds(0, 512)
    remote(w_left.at[half_rows], w_far.at[half_rows], x_send.at[2], wf_sem.at[0], right).wait_send()
    remote(w_left.at[half_rows], w_far.at[half_rows], x_send.at[3], wf_sem.at[0], left).wait_send()
    for half in range(2):
        @pl.when(jnp.logical_not(jnp.logical_and(owner_y == y, c == half)))
        def _():
            ref = scaled.at[pl.ds(half * 128, 128), :]
            remote(ref, ref, b_send.at[half], b_recv.at[0], sibling).wait_send()
    for way in range(2):
        @pl.when(is_source)
        def _():
            remote(cots.at[0], cots.at[0], z_send.at[way], sib_sem, sibling).wait_send()

        @pl.when(jnp.logical_not(is_source))
        def _():
            ref = cots.at[0, 0:768, :]
            remote(ref, ref, z_send.at[way], sib_sem, sibling).wait_send()
    remote(cots.at[0:2], cots.at[0:2], z_send.at[2], sib_sem, sibling).wait_send()


VMEM = pl.BlockSpec(memory_space=pltpu.VMEM)
HBM = pl.BlockSpec(memory_space=pltpu.HBM)


def body(activations, angles, clip_bits, codes, exponents, cotangent):
    dma = pltpu.SemaphoreType.DMA
    return pl.pallas_call(
        all_kernel,
        out_shape=(
            jax.ShapeDtypeStruct((256, 1024), BF16),
            jax.ShapeDtypeStruct((14, 512), F32),
        ),
        in_specs=[HBM] * 6,
        out_specs=(VMEM,) * 2,
        scratch_shapes=[
            pltpu.VMEM((16, 1024), jnp.int32),
            pltpu.VMEM((1, 640), jnp.int32),
            pltpu.VMEM((256, 640), BF16),
            pltpu.VMEM((14, 512), F32),
            pltpu.VMEM((1024, 640), BF16),
            pltpu.VMEM((256, 640), BF16),
            pltpu.VMEM((4, 1024, 640), BF16),
            pltpu.VMEM((1024, 640), BF16),
            pltpu.VMEM((1024, 640), BF16),
            pltpu.VMEM((1024, 640), BF16),
            pltpu.VMEM((CHUNKS, 3, 256, CHUNK), BF16),
            pltpu.VMEM((CHUNKS, 3, 256, CHUNK), BF16),
            pltpu.VMEM((CHUNKS, 256, CHUNK), F32),
            pltpu.VMEM((256, 1024), F32),
            pltpu.VMEM((256, 1024), BF16),
            pltpu.VMEM((2, 8, 16, 512), F32),
            pltpu.VMEM((14, 8, 16, 128), F32),
            pltpu.VMEM((14, 8, 16, 128), F32),
            pltpu.VMEM((14, 256, 1024), F32),
            pltpu.VMEM((7, 8, 16, 128), F32),
            pltpu.VMEM((7, 4, 16, 128), F32),
            pltpu.VMEM((256, 1024), F32),
            pltpu.VMEM((256, 1024), BF16),
            pltpu.VMEM((14, 16, 512), F32),
            pltpu.VMEM((16, 16, 512), F32),
            pltpu.VMEM((16, 1, 512), F32),
            pltpu.VMEM((16, 1, 512), F32),
            pltpu.VMEM((16, 1, 512), F32),
            dma((6,)), dma((4,)), dma((CHUNKS,)), dma((CHUNKS,)), dma((CHUNKS,)),
            dma((2,)), dma((4,)), dma((3,)), dma((4, 4)), dma((4, 4)), dma,
            dma, dma((CHUNKS,)), dma, dma, dma, dma, dma, dma, dma, dma,
            dma, dma, dma, dma, dma, dma, dma, dma,
        ],
        compiler_params=pltpu.CompilerParams(
            collective_id=0, has_side_effects=True, vmem_limit_bytes=56 * 2**20
        ),
        cost_estimate=pl.CostEstimate(flops=5400000000, bytes_accessed=6000000, transcendentals=0),
    )(activations, clip_bits, codes, exponents[None, :], cotangent, angles)


def solution(mesh):
    placed = (
        P("dp", "tensor"),
        P(None, "tensor"),
        P("dp", "tensor"),
        P("tensor", "dp"),
        P(),
        P("dp", "tensor"),
    )
    return jax.shard_map(
        body,
        mesh=mesh,
        in_specs=placed,
        out_specs=(P("dp", "tensor"), P(None, "tensor")),
        check_vma=False,
    )
```

time: 151 us -> 131 us (0.87)
  Pallas kernels: 143 us -> 127 us
  local copies, waits for them, and re-layouts: 7.11 us -> 3.24 us
    pallas_call x3 -> x1, Pallas kernels: 143 us -> 127 us  [body(): pl.pallas_call(all_kernel, out_shape=(jax.ShapeDtypeStruct((256, 1024), B...]
    unnamed x14 -> x2, local copies, waits for them, and re-layouts: 7.11 us -> 3.24 us
where the time goes in v2:
time: 131 us
  Pallas kernels  127 us (97%)
  local copies, waits for them, and re-layouts  3.24 us (2%)
    pallas_call x1, Pallas kernels, body(): pl.pallas_call(all_kernel, out_shape=(jax.ShapeDtypeStruct((256, 1024), B...  127 us
    unnamed x2, local copies, waits for them, and re-layouts  3.24 us

profile of v2, /device:TPU:1, one launch (start us, length us, event | category | flops | bytes accessed | tf_op | source)
XLA Modules:
  0.0 131.1 jit_solution(9355512729301900766)
XLA Ops:
  0.6 127.2 %shard_map.77 = (bf16[256,1024]{1,0:T(8,128)(2,1)}, f32[14,512]{1,0:T(8,128)}) custom-call(bf16[256,1024]{1,0:T(8,128)(2,1)} %acts.1, s32[16,1024]{1,0:T(8,128)} %clip.1, bf16[1024,640]{1,0:T(8,128)(2,1)} %codes.1, s32[1,10240]{1,0:T(1,128)} %bitcast.1, bf16[256,640]{1,0:T(8,128)(2,1)} %cot.1, f32[14,512]{1,0:T(8,128)} %angles.1), custom_call_target="tpu_custom_call" | custom-call | flops 5400000000 | bytes 6000000 | tf_op jit(solution)/shard_map/pallas_call | solution.py:539
  127.9 1.9 %copy.10 = bf16[256,1024]{1,0:T(8,128)(2,1)} copy(bf16[256,1024]{1,0:T(8,128)(2,1)} %get-tuple-element.4) | data formatting | bytes 1048576
  129.7 1.4 %copy.11 = f32[14,512]{1,0:T(8,128)} copy(f32[14,512]{1,0:T(8,128)} %get-tuple-element.5) | data formatting | bytes 57344

commit v3 on v2

--- a/solution.py
+++ b/solution.py
@@ -10,6 +10,7 @@
 BF16 = jnp.bfloat16
 CHUNK = 256
 CHUNKS = 4
+ORDER = (2, 1, 3, 0)
 
 
 def place():
@@ -66,11 +67,11 @@
     acts, clip, codes, exps, cot, angles,
     out, angle_out,
     clip_v, exps_v, cot_v, ang_v, w_own,
-    scaled, cots, w_left, w_right, w_far, sent, got, whole,
+    scaled, cots, w_left, w_right, w_far, sent, got, steps, got_steps, whole, narrow,
     q_in, a_in, ang, cos_t, sin_t, states, terms, tops, tall, q_back,
     parts, by_tokens, row_out, by_width, final,
     l_sem, x_send, wl_sem, wr_sem, wf_sem, b_send, b_recv, z_send, up_sem, down_sem, sib_sem,
-    d_send, d_recv, e_send, e_recv, f_send, f_recv, g_send, g_recv, h_send, h_recv,
+    s_send, s_recv, d_send, d_recv, e_send, e_recv, f_send, f_recv, g_send, g_recv, h_send, h_recv,
     o_send, o_recv, p_send, p_recv, r_send, r_recv, t_send, t_recv,
 ):
     d, k, x, y, z, c = place()
@@ -167,43 +168,49 @@
             ang.at[c, z], ang.at[c, z], g_send, g_recv, (d, ((z + i) % 8) * 2 + c)
         ).start()
 
-    def to_sibling(ref):
-        remote(ref, ref, z_send.at[2], sib_sem, sibling).start()
+    def to_sibling(ref, n):
+        remote(ref, ref, z_send.at[2], sib_sem.at[n], sibling).start()
 
     is_source = (z % 2) == (y // 2)
+
+    def group(n):
+        return (y + ORDER[n]) % 4
 
     @pl.when(is_source)
     def _():
-        for g in range(4):
+        for n in range(4):
+            g = group(n)
             ref = piece(z // 2, g, c)
 
             @pl.when(jnp.logical_not(jnp.logical_and(y == g, y % 2 == c)))
             def _():
                 remote(ref, ref, b_send.at[0], b_recv.at[g], sibling).wait_recv()
 
-            remote(ref, ref, z_send.at[0], up_sem.at[0, g], up).start()
-            remote(ref, ref, z_send.at[1], down_sem.at[0, g], down).start()
-            to_sibling(ref)
-
-    def pass_on(t):
+            remote(ref, ref, z_send.at[0], up_sem.at[0, n], up).start()
+            remote(ref, ref, z_send.at[1], down_sem.at[0, n], down).start()
+            to_sibling(ref, n)
+
+    def pass_on(t, n):
         below = (z + 8 - t) % 8
         above = (z + t) % 8
 
         @pl.when((below % 2) == (y // 2))
         def _():
-            for g in range(4):
-                if t < 4 or g < 2:
-                    ref = piece(below // 2, g, c)
-                    remote(ref, ref, z_send.at[0], up_sem.at[t - 1, g], up).wait_recv()
-                    if t < 3 or (t == 3 and g < 2):
-                        remote(ref, ref, z_send.at[0], up_sem.at[t, g], up).start()
-                    to_sibling(ref)
-                if t < 4 or g >= 2:
-                    ref = piece(above // 2, g, c)
-                    remote(ref, ref, z_send.at[1], down_sem.at[t - 1, g], down).wait_recv()
-                    if t < 3 or (t == 3 and g >= 2):
-                        remote(ref, ref, z_send.at[1], down_sem.at[t, g], down).start()
-                    to_sibling(ref)
+            if t < 4 or n % 2 == 0:
+                ref = piece(below // 2, group(n), c)
+                remote(ref, ref, z_send.at[0], up_sem.at[t - 1, n], up).wait_recv()
+                if t < 3 or (t == 3 and n % 2 == 0):
+                    remote(ref, ref, z_send.at[0], up_sem.at[t, n], up).start()
+                to_sibling(ref, n)
+            if t < 4 or n % 2 == 1:
+                ref = piece(above // 2, group(n), c)
+                remote(ref, ref, z_send.at[1], down_sem.at[t - 1, n], down).wait_recv()
+                if t < 3 or (t == 3 and n % 2 == 1):
+                    remote(ref, ref, z_send.at[1], down_sem.at[t, n], down).start()
+                to_sibling(ref, n)
+
+    def group_here(n):
+        remote(cots.at[0, 0:512, :], cots.at[0, 0:512, :], z_send.at[2], sib_sem.at[n], sibling).wait_recv()
 
     def forward(f):
         rows = pl.ds(f * CHUNK, CHUNK)
@@ -214,46 +221,130 @@
             remote(w_right.at[rows], w_right.at[rows], x_send.at[1], wr_sem.at[f], left).wait_recv()
             remote(w_right.at[rows], w_far.at[rows], x_send.at[3], wf_sem.at[f], left).start()
 
-    pass_on(1)
-    pass_on(2)
+    def chunk_here(f):
+        rows = pl.ds(f * CHUNK, CHUNK)
+        if f % 2 == 1:
+            remote(w_left.at[rows], w_left.at[rows], x_send.at[0], wl_sem.at[f], right).wait_recv()
+        else:
+            remote(w_right.at[rows], w_right.at[rows], x_send.at[1], wr_sem.at[f], left).wait_recv()
+        remote(w_far.at[rows], w_far.at[rows], x_send.at[2], wf_sem.at[f], right).wait_recv()
+
+    def product(f, n):
+        rows = pl.ds(pl.multiple_of(f * CHUNK, CHUNK), CHUNK)
+        to_y = (y + jnp.where(n == 3, 0, jnp.where(n == 0, 2, jnp.where(n == 1, 1, 3)))) % 4
+        tokens = pl.ds(pl.multiple_of(to_y * 256, 256), 256)
+
+        def part(index, ref):
+            return lax.dot_general(
+                cots[index, tokens, :], ref[rows, :], (((1,), (1,)), ((), ())),
+                preferred_element_type=F32,
+            )
+
+        total = part(x, w_own)
+        total = total + part((x + 3) % 4, w_left)
+        total = total + part((x + 1) % 4, w_right)
+        return to_y, total + part((x + 2) % 4, w_far)
+
+    def to_row(f, n):
+        to_y, total = product(f, n)
+        most = jnp.max(jnp.max(jnp.abs(total), axis=0, keepdims=True), axis=1, keepdims=True)
+        most = jnp.maximum(most, 1e-30)
+        sent[f, n] = jnp.round(total * (32000.0 / most)).astype(jnp.int32).astype(jnp.int16)
+        steps[f, n] = jnp.broadcast_to(most * (1.0 / 32000.0), (1, 128))
+        remote(steps.at[f, n], got_steps.at[f, n], s_send, s_recv.at[f], dev(x, to_y, z, c)).start()
+        remote(sent.at[f, n], got.at[f, n], d_send, d_recv.at[f], dev(x, to_y, z, c)).start()
+
+    lane_row = lax.broadcasted_iota(jnp.int32, (128, 128), 1)
+    lane_col = lax.broadcasted_iota(jnp.int32, (128, 128), 0)
+
+    def low_tables(first, last):
+        for s in range(first, last):
+            rows = jnp.concatenate(
+                [ang[core, :, s, a * 128 : (a + 1) * 128] for a in range(4) for core in range(2)], axis=0
+            )
+            for b in range(2):
+                pick = jnp.where(lane_col == b * 64 + squeezed(lane_row, s), 1.0, 0.0)
+                theta = jnp.dot(rows, pick, precision=lax.Precision.HIGHEST, preferred_element_type=F32)
+                sine, cosine = sine_cosine(theta)
+                upper = (lax.broadcasted_iota(jnp.int32, theta.shape, 1) & (1 << s)) != 0
+                signed = jnp.where(upper, sine, -sine)
+                for a in range(4):
+                    cos_t[s, 2 * a + b] = cosine[a * 16 : (a + 1) * 16]
+                    sin_t[s, 2 * a + b] = signed[a * 16 : (a + 1) * 16]
+
+    def high_tables():
+        for s in range(7, 14):
+            for a in range(4):
+                for core in range(2):
+                    sine, cosine = sine_cosine(ang[core, :, s, a * 128 : (a + 1) * 128])
+                    cos_t[s, a, core * 8 : core * 8 + 8] = cosine
+                    sin_t[s, a, core * 8 : core * 8 + 8] = sine
+
+    pass_on(1, 0)
+    pass_on(2, 0)
+    pass_on(1, 1)
     forward(0)
     forward(1)
-    pass_on(3)
-    send_activations()
-
+    pass_on(3, 0)
     remote(ang.at[0, 0:7], ang.at[0, 0:7], g_send, g_recv, sibling).wait_recv()
     remote(ang.at[c], ang.at[c], h_send, h_recv, sibling).start()
+    pass_on(2, 1)
+    pass_on(4, 0)
+    pass_on(1, 2)
+    remote(ang.at[0], ang.at[0], h_send, h_recv, sibling).wait_recv()
+    pass_on(3, 1)
+    loads[3].wait()
+    loads[4].wait()
+    own_copy.wait()
+    group_here(0)
+    chunk_here(0)
+    to_row(0, 0)
     forward(2)
+    pass_on(2, 2)
+    chunk_here(1)
+    to_row(1, 0)
+    pass_on(4, 1)
     forward(3)
-    pass_on(4)
-    remote(ang.at[0], ang.at[0], h_send, h_recv, sibling).wait_recv()
-    lane_row = lax.broadcasted_iota(jnp.int32, (128, 128), 1)
-    lane_col = lax.broadcasted_iota(jnp.int32, (128, 128), 0)
-    for s in range(7):
-        rows = jnp.concatenate(
-            [ang[core, :, s, a * 128 : (a + 1) * 128] for a in range(4) for core in range(2)], axis=0
-        )
-        for b in range(2):
-            pick = jnp.where(lane_col == b * 64 + squeezed(lane_row, s), 1.0, 0.0)
-            theta = jnp.dot(rows, pick, precision=lax.Precision.HIGHEST, preferred_element_type=F32)
-            sine, cosine = sine_cosine(theta)
-            upper = (lax.broadcasted_iota(jnp.int32, theta.shape, 1) & (1 << s)) != 0
-            signed = jnp.where(upper, sine, -sine)
-            for a in range(4):
-                cos_t[s, 2 * a + b] = cosine[a * 16 : (a + 1) * 16]
-                sin_t[s, 2 * a + b] = signed[a * 16 : (a + 1) * 16]
-    for s in range(7, 14):
-        for a in range(4):
-            for core in range(2):
-                sine, cosine = sine_cosine(ang[core, :, s, a * 128 : (a + 1) * 128])
-                cos_t[s, a, core * 8 : core * 8 + 8] = cosine
-                sin_t[s, a, core * 8 : core * 8 + 8] = sine
-
-
-    remote(cots.at[0:2], cots.at[0:2], z_send.at[2], sib_sem, sibling).wait_recv()
+    pass_on(1, 3)
+    low_tables(0, 2)
+    pass_on(3, 2)
+    group_here(1)
+
+    @pl.loop(0, 2)
+    def _(f):
+        to_row(f, 1)
+
+    pass_on(2, 3)
+    low_tables(2, 4)
+    pass_on(4, 2)
+    pass_on(3, 3)
+    send_activations()
+    low_tables(4, 7)
+    chunk_here(2)
+
+    @pl.loop(0, 2)
+    def _(n):
+        to_row(2, n)
+
+    group_here(2)
+
+    @pl.loop(0, 3)
+    def _(f):
+        to_row(f, 2)
+
+    pass_on(4, 3)
+    high_tables()
+    chunk_here(3)
+
+    @pl.loop(0, 3)
+    def _(n):
+        to_row(3, n)
+
+    group_here(3)
 
     def finish(f):
         lanes = pl.ds(pl.multiple_of(f * CHUNK, CHUNK), CHUNK)
+        remote(steps.at[f], got_steps.at[f], s_send, s_recv.at[f], sibling).wait_recv()
         remote(got.at[f], got.at[f], d_send, d_recv.at[f], sibling).wait_recv()
         place_in_word = lax.broadcasted_iota(jnp.int32, (16, CHUNK), 0)
 
@@ -261,7 +352,8 @@
             rows = pl.ds(pl.multiple_of(w * 16, 16), 16)
             total = whole[f, rows, :]
             for j in range(3):
-                total = total + got[f, j, rows, :].astype(F32)
+                step = jnp.concatenate([got_steps[f, j], got_steps[f, j]], axis=1)
+                total = total + got[f, j, rows, :].astype(jnp.int32).astype(F32) * step
             word = jnp.broadcast_to(clip_v[pl.ds(w, 1), lanes], (16, CHUNK))
             bit = jnp.bitwise_and(jnp.right_shift(word, place_in_word), 1)
             return rows, jnp.where(bit == 1, total, 0.0)
@@ -270,65 +362,19 @@
         def _(i):
             to = (k + i) % 16
             rows, value = masked(to)
-            whole[f, rows, :] = value
+            narrow[f, rows, :] = value.astype(BF16)
             remote(
-                whole.at[f, rows, :], q_in.at[mine16, lanes], e_send, e_recv, (d, to)
+                narrow.at[f, rows, :], q_in.at[mine16, lanes], e_send, e_recv, (d, to)
             ).start()
 
         _, value = masked(k)
-        q_in[mine16, lanes] = value
-
-    loads[3].wait()
-    loads[4].wait()
-    own_copy.wait()
-
-    @pl.loop(0, 4 * CHUNKS)
-    def _(i):
-        f = i // 4
-        j = i % 4
-        to_y = (y + j + 1) % 4
-        rows = pl.ds(pl.multiple_of(f * CHUNK, CHUNK), CHUNK)
-        tokens = pl.ds(pl.multiple_of(to_y * 256, 256), 256)
-
-        @pl.when(j == 0)
-        def _():
-            @pl.when(f % 2 == 1)
-            def _():
-                remote(w_left.at[rows], w_left.at[rows], x_send.at[0], wl_sem.at[f], right).wait_recv()
-
-            @pl.when(f % 2 == 0)
-            def _():
-                remote(w_right.at[rows], w_right.at[rows], x_send.at[1], wr_sem.at[f], left).wait_recv()
-
-            remote(w_far.at[rows], w_far.at[rows], x_send.at[2], wf_sem.at[f], right).wait_recv()
-
-        def product(part, ref):
-            return lax.dot_general(
-                cots[part, tokens, :], ref[rows, :], (((1,), (1,)), ((), ())),
-                preferred_element_type=F32,
-            )
-
-        total = product(x, w_own)
-        total = total + product((x + 3) % 4, w_left)
-        total = total + product((x + 1) % 4, w_right)
-        total = total + product((x + 2) % 4, w_far)
-
-        @pl.when(j < 3)
-        def _():
-            sent[f, j] = total.astype(BF16)
-            remote(
-                sent.at[f, j], got.at[f, j], d_send, d_recv.at[f], dev(x, to_y, z, c)
-            ).start()
-
-        @pl.when(j == 3)
-        def _():
-            whole[f] = total
-
-            @pl.when(f > 0)
-            def _():
-                finish(f - 1)
-
-    finish(CHUNKS - 1)
+        q_in[mine16, lanes] = value.astype(BF16)
+
+    @pl.loop(0, CHUNKS)
+    def _(f):
+        _, total = product(f, 3)
+        whole[f] = total
+        finish(f)
 
     remote(a_in.at[0:240], a_in.at[0:240], f_send, f_recv, sibling).wait()
 
@@ -357,11 +403,10 @@
                 states[s, rows, t * 128 : (t + 1) * 128] = field[t]
 
     def fixed_row(table, s, t, m):
-        return jnp.broadcast_to(table[s, t % 4, pl.ds((t // 4) * 8 + m, 1), :], (8, 128))
+        return jnp.broadcast_to(table[s, t % 4, pl.ds((t // 4) * 8 + m, 1), :], (16, 128))
 
     def halves(lo, hi):
-        for half in range(2):
-            yield slice(lo * 16 + half * 8, lo * 16 + half * 8 + 8), slice(hi * 16 + half * 8, hi * 16 + half * 8 + 8)
+        yield slice(lo * 16, lo * 16 + 16), slice(hi * 16, hi * 16 + 16)
 
     @pl.loop(0, 8)
     def _(t):
@@ -394,7 +439,7 @@
                 cosine, sine = fixed_row(cos_t, s, t, m), fixed_row(sin_t, s, t, m)
                 total = None
                 for lo_rows, hi_rows in halves(lo, hi):
-                    q_lo, q_hi = source[lo_rows, lanes], source[hi_rows, lanes]
+                    q_lo, q_hi = source[lo_rows, lanes].astype(F32), source[hi_rows, lanes].astype(F32)
                     term = q_hi * states[s, lo_rows, lanes] - q_lo * states[s, hi_rows, lanes]
                     total = term if total is None else total + term
                     tall[lo_rows, lanes] = cosine * q_lo + sine * q_hi
@@ -455,8 +500,12 @@
         for b in range(2):
             pick = jnp.where(lane_row == b * 64 + squeezed(lane_col, s), sign, 0.0)
             rows = jnp.concatenate([terms[s, 2 * a + b] for a in range(4)], axis=0)
-            part = jnp.dot(rows, pick, precision=lax.Precision.HIGHEST, preferred_element_type=F32)
-            total = part if total is None else total + part
+            pick = pick.astype(BF16)
+            for _ in range(3):
+                high = rows.astype(BF16)
+                part = jnp.dot(high, pick, preferred_element_type=F32)
+                total = part if total is None else total + part
+                rows = rows - high.astype(F32)
         for a in range(4):
             parts[s, :, a * 128 : (a + 1) * 128] = total[a * 16 : (a + 1) * 16]
 
@@ -507,6 +556,7 @@
     remote(q_back.at[0:240], out.at[0:240], o_send, o_recv, sibling).wait()
     remote(ang.at[0, 0:7], ang.at[0, 0:7], g_send, g_recv, sibling).wait_send()
     remote(ang.at[0], ang.at[0], h_send, h_recv, sibling).wait_send()
+    remote(steps, got_steps, s_send, s_recv.at[0], sibling).wait_send()
     remote(sent, got, d_send, d_recv.at[0], sibling).wait_send()
     remote(w_own, w_left, x_send.at[0], wl_sem.at[0], right).wait_send()
     remote(w_own, w_right, x_send.at[1], wr_sem.at[0], left).wait_send()
@@ -521,13 +571,13 @@
     for way in range(2):
         @pl.when(is_source)
         def _():
-            remote(cots.at[0], cots.at[0], z_send.at[way], sib_sem, sibling).wait_send()
+            remote(cots.at[0], cots.at[0], z_send.at[way], sib_sem.at[0], sibling).wait_send()
 
         @pl.when(jnp.logical_not(is_source))
         def _():
             ref = cots.at[0, 0:768, :]
-            remote(ref, ref, z_send.at[way], sib_sem, sibling).wait_send()
-    remote(cots.at[0:2], cots.at[0:2], z_send.at[2], sib_sem, sibling).wait_send()
+            remote(ref, ref, z_send.at[way], sib_sem.at[0], sibling).wait_send()
+    remote(cots.at[0:2], cots.at[0:2], z_send.at[2], sib_sem.at[0], sibling).wait_send()
 
 
 VMEM = pl.BlockSpec(memory_space=pltpu.VMEM)
@@ -555,10 +605,13 @@
             pltpu.VMEM((1024, 640), BF16),
             pltpu.VMEM((1024, 640), BF16),
             pltpu.VMEM((1024, 640), BF16),
-            pltpu.VMEM((CHUNKS, 3, 256, CHUNK), BF16),
-            pltpu.VMEM((CHUNKS, 3, 256, CHUNK), BF16),
+            pltpu.VMEM((CHUNKS, 3, 256, CHUNK), jnp.int16),
+            pltpu.VMEM((CHUNKS, 3, 256, CHUNK), jnp.int16),
+            pltpu.VMEM((CHUNKS, 3, 1, 128), F32),
+            pltpu.VMEM((CHUNKS, 3, 1, 128), F32),
             pltpu.VMEM((CHUNKS, 256, CHUNK), F32),
-            pltpu.VMEM((256, 1024), F32),
+            pltpu.VMEM((CHUNKS, 256, CHUNK), BF16),
+            pltpu.VMEM((256, 1024), BF16),
             pltpu.VMEM((256, 1024), BF16),
             pltpu.VMEM((2, 8, 16, 512), F32),
             pltpu.VMEM((14, 8, 16, 128), F32),
@@ -574,8 +627,8 @@
             pltpu.VMEM((16, 1, 512), F32),
             pltpu.VMEM((16, 1, 512), F32),
             dma((6,)), dma((4,)), dma((CHUNKS,)), dma((CHUNKS,)), dma((CHUNKS,)),
-            dma((2,)), dma((4,)), dma((3,)), dma((4, 4)), dma((4, 4)), dma,
-            dma, dma((CHUNKS,)), dma, dma, dma, dma, dma, dma, dma, dma,
+            dma((2,)), dma((4,)), dma((3,)), dma((4, 4)), dma((4, 4)), dma((4,)),
+            dma, dma((CHUNKS,)), dma, dma((CHUNKS,)), dma, dma, dma, dma, dma, dma, dma, dma,
             dma, dma, dma, dma, dma, dma, dma, dma,
         ],
         compiler_params=pltpu.CompilerParams(

time: 131 us -> 123 us (0.939)
  Pallas kernels: 127 us -> 118 us
    pallas_call x1, Pallas kernels: 127 us -> 118 us  [body(): pl.pallas_call(all_kernel, out_shape=(jax.ShapeDtypeStruct((256, 1024), B...]
where the time goes in v3:
time: 123 us; the launch traced here: 122 us
  Pallas kernels  118 us (96%)
  local copies, waits for them, and re-layouts  3.24 us (3%)
    pallas_call x1, Pallas kernels, body(): pl.pallas_call(all_kernel, out_shape=(jax.ShapeDtypeStruct((256, 1024), B...  118 us
    unnamed x2, local copies, waits for them, and re-layouts  3.24 us

profile of v3, /device:TPU:1, one launch (start us, length us, event | category | flops | bytes accessed | tf_op | source)
XLA Modules:
  0.0 122.4 jit_solution(11407395348896136852)
XLA Ops:
  0.6 118.5 %shard_map.77 = (bf16[256,1024]{1,0:T(8,128)(2,1)}, f32[14,512]{1,0:T(8,128)}) custom-call(bf16[256,1024]{1,0:T(8,128)(2,1)} %acts.1, s32[16,1024]{1,0:T(8,128)} %clip.1, bf16[1024,640]{1,0:T(8,128)(2,1)} %codes.1, s32[1,10240]{1,0:T(1,128)} %bitcast.1, bf16[256,640]{1,0:T(8,128)(2,1)} %cot.1, f32[14,512]{1,0:T(8,128)} %angles.1), custom_call_target="tpu_custom_call" | custom-call | flops 5400000000 | bytes 6000000 | tf_op jit(solution)/shard_map/pallas_call | solution.py:589
  119.1 1.9 %copy.10 = bf16[256,1024]{1,0:T(8,128)(2,1)} copy(bf16[256,1024]{1,0:T(8,128)(2,1)} %get-tuple-element.4) | data formatting | bytes 1048576
  121.0 1.4 %copy.11 = f32[14,512]{1,0:T(8,128)} copy(f32[14,512]{1,0:T(8,128)} %get-tuple-element.5) | data formatting | bytes 57344

commit v4 on v3

--- a/solution.py
+++ b/solution.py
@@ -70,7 +70,7 @@
     scaled, cots, w_left, w_right, w_far, sent, got, steps, got_steps, whole, narrow,
     q_in, a_in, ang, cos_t, sin_t, states, terms, tops, tall, q_back,
     parts, by_tokens, row_out, by_width, final,
-    l_sem, x_send, wl_sem, wr_sem, wf_sem, b_send, b_recv, z_send, up_sem, down_sem, sib_sem,
+    l_sem, x_send, wl_sem, wr_sem, wf_sem, b_send, b_recv, own_send, z_send, up_sem, down_sem, sib_sem,
     s_send, s_recv, d_send, d_recv, e_send, e_recv, f_send, f_recv, g_send, g_recv, h_send, h_recv,
     o_send, o_recv, p_send, p_recv, r_send, r_recv, t_send, t_recv,
 ):
@@ -122,10 +122,13 @@
                 acts.at[pl.ds(pl.multiple_of(to * 16, 16), 16), :], a_in.at[mine16, :], f_send, f_recv, (d, to)
             ).start()
 
-    for f in range(CHUNKS):
+    def send_codes(f):
         rows = pl.ds(f * CHUNK, CHUNK)
         remote(codes.at[rows], w_left.at[rows], x_send.at[0], wl_sem.at[f], right).start()
         remote(codes.at[rows], w_right.at[rows], x_send.at[1], wr_sem.at[f], left).start()
+
+    send_codes(0)
+    send_codes(1)
 
     for n in range(3):
         loads[n].wait()
@@ -176,19 +179,32 @@
     def group(n):
         return (y + ORDER[n]) % 4
 
+    def own_copies(n):
+        ref = piece(z // 2, group(n), c)
+        return (
+            remote(ref, ref, own_send.at[0, n], up_sem.at[0, n], up),
+            remote(ref, ref, own_send.at[1, n], down_sem.at[0, n], down),
+        )
+
+    def send_own(n):
+        g = group(n)
+        ref = piece(z // 2, g, c)
+
+        @pl.when(jnp.logical_not(jnp.logical_and(y == g, y % 2 == c)))
+        def _():
+            remote(ref, ref, b_send.at[0], b_recv.at[g], sibling).wait_recv()
+
+        if n > 0:
+            for copy in own_copies(n - 1):
+                copy.wait_send()
+        for copy in own_copies(n):
+            copy.start()
+        to_sibling(ref, n)
+
     @pl.when(is_source)
     def _():
-        for n in range(4):
-            g = group(n)
-            ref = piece(z // 2, g, c)
-
-            @pl.when(jnp.logical_not(jnp.logical_and(y == g, y % 2 == c)))
-            def _():
-                remote(ref, ref, b_send.at[0], b_recv.at[g], sibling).wait_recv()
-
-            remote(ref, ref, z_send.at[0], up_sem.at[0, n], up).start()
-            remote(ref, ref, z_send.at[1], down_sem.at[0, n], down).start()
-            to_sibling(ref, n)
+        for n in range(3):
+            send_own(n)
 
     def pass_on(t, n):
         below = (z + 8 - t) % 8
@@ -282,13 +298,20 @@
 
     pass_on(1, 0)
     pass_on(2, 0)
+
+    @pl.when(is_source)
+    def _():
+        send_own(3)
+
     pass_on(1, 1)
     forward(0)
     forward(1)
     pass_on(3, 0)
     remote(ang.at[0, 0:7], ang.at[0, 0:7], g_send, g_recv, sibling).wait_recv()
     remote(ang.at[c], ang.at[c], h_send, h_recv, sibling).start()
+    send_codes(2)
     pass_on(2, 1)
+    send_codes(3)
     pass_on(4, 0)
     pass_on(1, 2)
     remote(ang.at[0], ang.at[0], h_send, h_recv, sibling).wait_recv()
@@ -296,15 +319,13 @@
     loads[3].wait()
     loads[4].wait()
     own_copy.wait()
+    pass_on(2, 2)
     group_here(0)
     chunk_here(0)
     to_row(0, 0)
-    forward(2)
-    pass_on(2, 2)
+    pass_on(4, 1)
     chunk_here(1)
     to_row(1, 0)
-    pass_on(4, 1)
-    forward(3)
     pass_on(1, 3)
     low_tables(0, 2)
     pass_on(3, 2)
@@ -314,32 +335,34 @@
     def _(f):
         to_row(f, 1)
 
+    forward(2)
     pass_on(2, 3)
+    forward(3)
     low_tables(2, 4)
     pass_on(4, 2)
     pass_on(3, 3)
     send_activations()
-    low_tables(4, 7)
+    group_here(2)
+
+    @pl.loop(0, 2)
+    def _(f):
+        to_row(f, 2)
+
     chunk_here(2)
 
-    @pl.loop(0, 2)
+    @pl.loop(0, 3)
     def _(n):
         to_row(2, n)
 
-    group_here(2)
-
-    @pl.loop(0, 3)
-    def _(f):
-        to_row(f, 2)
-
     pass_on(4, 3)
-    high_tables()
+    low_tables(4, 7)
     chunk_here(3)
 
     @pl.loop(0, 3)
     def _(n):
         to_row(3, n)
 
+    high_tables()
     group_here(3)
 
     def finish(f):
@@ -571,7 +594,9 @@
     for way in range(2):
         @pl.when(is_source)
         def _():
-            remote(cots.at[0], cots.at[0], z_send.at[way], sib_sem.at[0], sibling).wait_send()
+            ref = cots.at[0, 0:512, :]
+            remote(ref, ref, z_send.at[way], sib_sem.at[0], sibling).wait_send()
+            own_copies(3)[way].wait_send()
 
         @pl.when(jnp.logical_not(is_source))
         def _():
@@ -627,7 +652,7 @@
             pltpu.VMEM((16, 1, 512), F32),
             pltpu.VMEM((16, 1, 512), F32),
             dma((6,)), dma((4,)), dma((CHUNKS,)), dma((CHUNKS,)), dma((CHUNKS,)),
-            dma((2,)), dma((4,)), dma((3,)), dma((4, 4)), dma((4, 4)), dma((4,)),
+            dma((2,)), dma((4,)), dma((2, 4)), dma((3,)), dma((4, 4)), dma((4, 4)), dma((4,)),
             dma, dma((CHUNKS,)), dma, dma((CHUNKS,)), dma, dma, dma, dma, dma, dma, dma, dma,
             dma, dma, dma, dma, dma, dma, dma, dma,
         ],

time: 123 us -> 117 us (0.951)
  Pallas kernels: 118 us -> 113 us
    pallas_call x1, Pallas kernels: 118 us -> 113 us  [body(): pl.pallas_call(all_kernel, out_shape=(jax.ShapeDtypeStruct((256, 1024), B...]
where the time goes in v4:
time: 117 us
  Pallas kernels  113 us (97%)
  local copies, waits for them, and re-layouts  3.24 us (3%)
    pallas_call x1, Pallas kernels, body(): pl.pallas_call(all_kernel, out_shape=(jax.ShapeDtypeStruct((256, 1024), B...  113 us
    unnamed x2, local copies, waits for them, and re-layouts  3.24 us

profile of v4, /device:TPU:1, one launch (start us, length us, event | category | flops | bytes accessed | tf_op | source)
XLA Modules:
  0.0 116.6 jit_solution(1877503301102946729)
XLA Ops:
  0.6 112.8 %shard_map.77 = (bf16[256,1024]{1,0:T(8,128)(2,1)}, f32[14,512]{1,0:T(8,128)}) custom-call(bf16[256,1024]{1,0:T(8,128)(2,1)} %acts.1, s32[16,1024]{1,0:T(8,128)} %clip.1, bf16[1024,640]{1,0:T(8,128)(2,1)} %codes.1, s32[1,10240]{1,0:T(1,128)} %bitcast.1, bf16[256,640]{1,0:T(8,128)(2,1)} %cot.1, f32[14,512]{1,0:T(8,128)} %angles.1), custom_call_target="tpu_custom_call" | custom-call | flops 5400000000 | bytes 6000000 | tf_op jit(solution)/shard_map/pallas_call | solution.py:614
  113.4 1.9 %copy.10 = bf16[256,1024]{1,0:T(8,128)(2,1)} copy(bf16[256,1024]{1,0:T(8,128)(2,1)} %get-tuple-element.4) | data formatting | bytes 1048576
  115.3 1.4 %copy.11 = f32[14,512]{1,0:T(8,128)} copy(f32[14,512]{1,0:T(8,128)} %get-tuple-element.5) | data formatting | bytes 57344

commit v5 on v4

--- a/solution.py
+++ b/solution.py
@@ -341,7 +341,6 @@
     low_tables(2, 4)
     pass_on(4, 2)
     pass_on(3, 3)
-    send_activations()
     group_here(2)
 
     @pl.loop(0, 2)
@@ -363,6 +362,7 @@
         to_row(3, n)
 
     high_tables()
+    send_activations()
     group_here(3)
 
     def finish(f):

time: 117 us -> 124 us (1.060)
  Pallas kernels: 113 us -> 120 us
    pallas_call x1, Pallas kernels: 113 us -> 120 us  [body(): pl.pallas_call(all_kernel, out_shape=(jax.ShapeDtypeStruct((256, 1024), B...]
where the time goes in v5:
time: 124 us
  Pallas kernels  120 us (97%)
  local copies, waits for them, and re-layouts  3.24 us (3%)
    pallas_call x1, Pallas kernels, body(): pl.pallas_call(all_kernel, out_shape=(jax.ShapeDtypeStruct((256, 1024), B...  120 us
    unnamed x2, local copies, waits for them, and re-layouts  3.24 us

profile of v5, /device:TPU:1, one launch (start us, length us, event | category | flops | bytes accessed | tf_op | source)
XLA Modules:
  0.0 124.2 jit_solution(4399644035102417991)
XLA Ops:
  0.6 120.3 %shard_map.77 = (bf16[256,1024]{1,0:T(8,128)(2,1)}, f32[14,512]{1,0:T(8,128)}) custom-call(bf16[256,1024]{1,0:T(8,128)(2,1)} %acts.1, s32[16,1024]{1,0:T(8,128)} %clip.1, bf16[1024,640]{1,0:T(8,128)(2,1)} %codes.1, s32[1,10240]{1,0:T(1,128)} %bitcast.1, bf16[256,640]{1,0:T(8,128)(2,1)} %cot.1, f32[14,512]{1,0:T(8,128)} %angles.1), custom_call_target="tpu_custom_call" | custom-call | flops 5400000000 | bytes 6000000 | tf_op jit(solution)/shard_map/pallas_call | solution.py:614
  120.9 1.9 %copy.10 = bf16[256,1024]{1,0:T(8,128)(2,1)} copy(bf16[256,1024]{1,0:T(8,128)(2,1)} %get-tuple-element.4) | data formatting | bytes 1048576
  122.8 1.4 %copy.11 = f32[14,512]{1,0:T(8,128)} copy(f32[14,512]{1,0:T(8,128)} %get-tuple-element.5) | data formatting | bytes 57344
